TPU v7x, 256 devices: a whole 4x4x8 slice. The times are simulated.
256 devices in a mesh: dp: 32 (over z, x), hst: 8 (over y, core).
Axes of the slice: x: 4, y: 4, z: 8, core: 2. Of those that a mesh axis runs over, the one named last changes fastest.
Arguments:
- tokens: bfloat16 [512, 7168], P('dp', 'hst'), may hold values from -6 to 6
- cotangent: bfloat16 [512, 7168], P('dp', 'hst'), may hold values from -6 to 6
- expert_ids: int32 [512, 2], P('dp'), may hold values from 0 to 7, all different within a row; in each aligned block of 16 rows (0 to 15, 16 to 31, ...) at most 4 rows name the same one
- gate_values: float32 [512, 2], P('dp'), may hold values from 0.2 to 1
- w_gate: bfloat16 [8, 4864, 7168], P('hst', 'dp'), may hold values from -0.0625 to 0.0625
- w_up: bfloat16 [8, 4864, 7168], P('hst', 'dp'), may hold values from -0.0625 to 0.0625
- w_down: bfloat16 [8, 4864, 7168], P('hst', 'dp'), may hold values from -0.078125 to 0.078125
Outputs:
- mixed: bfloat16 [512, 7168], P('dp', 'hst')
- grad_tokens: bfloat16 [512, 7168], P('dp', 'hst')
- grad_gate: bfloat16 [8, 4864, 7168], P('hst', 'dp')
- grad_up: bfloat16 [8, 4864, 7168], P('hst', 'dp')
- grad_down: bfloat16 [8, 4864, 7168], P('hst', 'dp')
Inputs may be any that keep to these rules, and one draw needn't show every extreme that they name: `expert_ids`: within each block of 16 rows (the rows of one index of dp), a token names two different experts, and no expert is named by more than 4 routes; since a block has 32 routes and 32 slots, every expert fills all 4 of its slots in every block.
All inputs are finite; a program needn't handle non-finite values.
Results may differ from a plain program's by a relative error of at most 0.023.
Values may be sent and summed in bfloat16 or wider, within the bound.
A program may use at most 128 MiB of HBM per device.

v0:
```python
import jax
import jax.numpy as jnp
from jax import lax
from jax.sharding import PartitionSpec as P

CAP = 4


def route_tables(expert_ids, gate_values, experts, cap):
    count = expert_ids.shape[0]
    flat = expert_ids.reshape(-1)
    labels = jnp.arange(experts, dtype=jnp.int32)
    onehot = (flat[:, None] == labels[None, :]).astype(jnp.int32)
    position = jnp.cumsum(onehot, axis=0) - onehot
    slot = jnp.sum(position * onehot, axis=1)
    slots = jnp.arange(cap, dtype=jnp.int32)
    hit = (flat[:, None, None] == labels[None, :, None]) & (
        slot[:, None, None] == slots[None, None, :]
    )
    hit = hit.astype(jnp.float32).reshape(count, 2, experts, cap)
    select = jnp.transpose(jnp.sum(hit, axis=1), (1, 2, 0))
    weigh = jnp.transpose(jnp.sum(hit * gate_values[:, :, None, None], axis=1), (1, 2, 0))
    return (select, weigh)


def body(tokens, cotangent, expert_ids, gate_values, w_gate, w_up, w_down):
    highest = lax.Precision.HIGHEST
    hosts = lax.axis_size("hst")
    local = w_gate.shape[0]
    experts = local * hosts
    select, weigh = route_tables(expert_ids, gate_values, experts, CAP)
    first = lax.axis_index("hst") * local
    mine_select = lax.dynamic_slice_in_dim(select, first, local, 0)
    mine_weigh = lax.dynamic_slice_in_dim(weigh, first, local, 0)
    x_part = jnp.einsum(
        "ecT,Td->ecd", select.astype(jnp.bfloat16), tokens, preferred_element_type=jnp.float32
    ).astype(jnp.bfloat16)
    d_part = jnp.einsum(
        "ecT,Td->ecd", weigh, cotangent.astype(jnp.float32), precision=highest
    ).astype(jnp.bfloat16)
    x_rows, d_rows = (
        lax.all_to_all(x_part, "hst", split_axis=0, concat_axis=2, tiled=True),
        lax.all_to_all(d_part, "hst", split_axis=0, concat_axis=2, tiled=True),
    )
    x_all, d_all = (
        lax.all_gather(x_rows, "dp", axis=1, tiled=True),
        lax.all_gather(d_rows, "dp", axis=1, tiled=True),
    )
    gate_act = jnp.einsum("erd,efd->erf", x_all, w_gate, preferred_element_type=jnp.float32)
    up_act = jnp.einsum("erd,efd->erf", x_all, w_up, preferred_element_type=jnp.float32)
    sigma = jax.nn.sigmoid(gate_act)
    hidden = (gate_act * sigma * up_act).astype(jnp.bfloat16)
    out_terms = jnp.einsum("erf,efd->erd", hidden, w_down, preferred_element_type=jnp.float32)
    out_rows = lax.psum_scatter(
        out_terms.astype(jnp.bfloat16), "dp", scatter_dimension=1, tiled=True
    ).astype(jnp.float32)
    d_hidden = jnp.einsum("erd,efd->erf", d_all, w_down, preferred_element_type=jnp.float32)
    d_gate = (d_hidden * up_act * sigma * (1.0 + gate_act * (1.0 - sigma))).astype(jnp.bfloat16)
    d_up = (d_hidden * gate_act * sigma).astype(jnp.bfloat16)
    grad_down = jnp.einsum(
        "erf,erd->efd", hidden, d_all, preferred_element_type=jnp.float32
    ).astype(jnp.bfloat16)
    grad_gate = jnp.einsum(
        "erf,erd->efd", d_gate, x_all, preferred_element_type=jnp.float32
    ).astype(jnp.bfloat16)
    grad_up = jnp.einsum("erf,erd->efd", d_up, x_all, preferred_element_type=jnp.float32).astype(
        jnp.bfloat16
    )
    back_terms = jnp.einsum("erf,efd->erd", d_gate, w_gate, preferred_element_type=jnp.float32)
    back_terms = back_terms + jnp.einsum(
        "erf,efd->erd", d_up, w_up, preferred_element_type=jnp.float32
    )
    back_rows = lax.psum_scatter(
        back_terms.astype(jnp.bfloat16), "dp", scatter_dimension=1, tiled=True
    ).astype(jnp.float32)
    token_terms = jnp.einsum("ecT,ecd->Td", mine_weigh, out_rows, precision=highest)
    mixed = lax.psum_scatter(
        token_terms.astype(jnp.bfloat16), "hst", scatter_dimension=1, tiled=True
    )
    grad_terms = jnp.einsum("ecT,ecd->Td", mine_select, back_rows, precision=highest)
    grad_tokens = lax.psum_scatter(
        grad_terms.astype(jnp.bfloat16), "hst", scatter_dimension=1, tiled=True
    )
    return (mixed, grad_tokens, grad_gate, grad_up, grad_down)


def solution(mesh):
    return jax.shard_map(
        body,
        mesh=mesh,
        in_specs=(
            P("dp", "hst"),
            P("dp", "hst"),
            P("dp", None),
            P("dp", None),
            P("hst", "dp", None),
            P("hst", "dp", None),
            P("hst", "dp", None),
        ),
        out_specs=(
            P("dp", "hst"),
            P("dp", "hst"),
            P("hst", "dp", None),
            P("hst", "dp", None),
            P("hst", "dp", None),
        ),
        check_vma=False,
    )
```

profile of v0, /device:TPU:1, one launch (start us, length us, event | category | flops | bytes accessed | tf_op | source)
XLA Modules:
  0.0 430.5 jit_solution(2172842619272928740)
XLA Ops:
  7.2 0.9 copy.38
  9.4 0.7 fusion.25
  10.1 0.9 convolution_convert_fusion.7
  11.0 10.6 %all_to_all.36 = bf16[8,4,896]{2,1,0:T(4,128)(2,1)S(1)} all-to-all(bf16[8,4,896]{2,1,0:T(4,128)(2,1)S(1)} %copy.40), channel_id=1, replica_groups=mesh['dp'=32,'hst'=8] {'hst'}, dimensions={0} | all-to-all | bytes 114688 | tf_op jit(solution)/shard_map/all_to_all | solution.py:42
  21.6 0.7 copy.41
  22.4 0.9 convolution_convert_fusion.6
  23.4 7.9 %all_to_all.37 = bf16[8,4,896]{2,1,0:T(4,128)(2,1)S(1)} all-to-all(bf16[8,4,896]{2,1,0:T(4,128)(2,1)S(1)} %copy.42), channel_id=1, replica_groups=mesh['dp'=32,'hst'=8] {'hst'}, dimensions={0} | all-to-all | bytes 114688 | tf_op jit(solution)/shard_map/all_to_all | solution.py:43
  31.3 0.7 copy.43
  32.1 69.1 %all-gather.3.cloned.1.call-done = bf16[1,128,7168]{2,0,1:T(2,128)(2,1)} async-done(((bf16[1,4,7168]{2,0,1:T(2,128)(2,1)}), bf16[1,128,7168]{2,0,1:T(2,128)(2,1)}) %all-gather.3.cloned.1.call-update) | async-done | bytes 1835024 | tf_op jit(solution)/shard_map/all_gather | solution.py:46
  101.2 2.8 copy.52
  104.0 0.8 fusion.14
  105.2 1.0 copy-done.5
  106.2 0.8 fusion.10
  107.1 75.0 %all-gather.5.cloned.1.call-done = bf16[1,128,7168]{2,0,1:T(2,128)(2,1)} async-done(((bf16[1,4,7168]{2,0,1:T(2,128)(2,1)}), bf16[1,128,7168]{2,0,1:T(2,128)(2,1)}) %all-gather.5.cloned.1.call-update) | async-done | bytes 1835024 | tf_op jit(solution)/shard_map/all_gather | solution.py:47
  182.1 3.0 multiply_convert_fusion
  185.2 1.9 fusion.4
  187.1 0.7 fusion.12
  187.8 0.9 copy-done.6
  188.7 2.0 fusion.5
  192.7 156.0 %all-reduce.5.cloned.1.call-done = (bf16[1,128,7168]{2,1,0:T(8,128)(2,1)}, bf16[1,128,7168]{2,1,0:T(8,128)(2,1)}) async-done(((bf16[1,128,7168]{2,1,0:T(8,128)(2,1)}, bf16[1,128,7168]{2,1,0:T(8,128)(2,1)}), (bf16[1,128,7168]{2,1,0:T(8,128)(2,1)}, bf16[1,128,7168]{2,1,0:T(8,128)(2,1)})) %all-reduce.5.cloned.1.call-update) | async-done | bytes 3670032
  348.6 1.3 convolution_convert_fusion.5
  349.9 1.6 copy.46
  351.7 1.3 convolution_convert_fusion.4
  353.0 1.7 copy.50
  354.7 3.7 fusion.1
  358.4 2.1 fusion.2
  360.5 0.8 copy-done.7
  361.2 2.1 fusion.3
  363.4 22.0 %reduce-scatter.9.cloned.1.call-done = bf16[896,16]{1,0:T(8,128)(2,1)} async-done(((bf16[7168,16]{1,0:T(8,128)(2,1)}), bf16[896,16]{1,0:T(8,128)(2,1)}) %reduce-scatter.9.cloned.1.call-update) | async-done | bytes 28688
  385.3 1.7 copy.47
  387.0 35.3 %reduce-scatter.11.cloned.1.call-done = bf16[896,16]{1,0:T(8,128)(2,1)} async-done(((bf16[7168,16]{1,0:T(8,128)(2,1)}), bf16[896,16]{1,0:T(8,128)(2,1)}) %reduce-scatter.11.cloned.1.call-update) | async-done | bytes 28688
  422.3 1.7 copy.51
  (37 shorter events, 3.2 us)
Async XLA Ops:
  7.2 175.0 %copy-start = (bf16[1,152,7168]{2,1,0:T(8,128)(2,1)S(1)}, bf16[1,152,7168]{2,1,0:T(8,128)(2,1)}, u32[]{:S(2)}) copy-start(bf16[1,152,7168]{2,1,0:T(8,128)(2,1)} %param.13) | copy-start | bytes 6537220
  7.2 94.0 %all-gather.3.cloned.1.call-start = ((), (), s32[]{:S(2)}) async-start(), calls=%async_computation.4 | async-start | bytes 3784704 | tf_op jit(solution)/shard_map/all_gather | solution.py:46
  22.4 159.8 %all-gather.5.cloned.1.call-start = ((), (), s32[]{:S(2)}) async-start(), calls=%async_computation.5 | async-start | bytes 3784704 | tf_op jit(solution)/shard_map/all_gather | solution.py:47
  32.1 316.5 %all-reduce.5.cloned.1.call-start = ((), (), s32[]{:S(2)}) async-start(), calls=%async_computation.8 | async-start | bytes 7340032
  101.2 2.8 copy-start.3
  104.0 1.3 copy-start.1
  104.0 2.3 copy-start.5
  185.2 1.9 copy-start.4
  187.1 1.6 copy-start.6
  190.7 0.7 copy-start.8
  190.7 194.6 %reduce-scatter.9.cloned.1.call-start = ((), (), s32[]{:S(2)}) async-start(), calls=%async_computation.6 | async-start | bytes 2064384
  351.6 70.7 %reduce-scatter.11.cloned.1.call-start = ((), (), s32[]{:S(2)}) async-start(), calls=%async_computation.7 | async-start | bytes 2064384
  354.7 3.7 copy-start.2
  358.4 2.8 copy-start.7
Sparse Core Ops, SparseCore 0:
  22.5 78.6 all-gather.2
  104.3 77.7 all-gather.4
  190.9 157.7 all-reduce.4
  351.7 33.5 reduce-scatter.8
  387.8 34.5 reduce-scatter.10
where the time goes:
time: 433 us; the launch traced here: 430 us
  waiting for transfers between devices  357 us (82%)
  matrix products  21.7 us (5%)
  blocking collectives  18.5 us (4%)
  local copies, waits for them, and re-layouts  16.3 us (4%)
  between operations  14.6 us (3%)
    unnamed x8, waiting for transfers between devices  213 us
    all_gather x1, waiting for transfers between devices, body(): lax.all_gather(d_rows, 'dp', axis=1, tiled=True)  75 us
    all_gather x1, waiting for transfers between devices, body(): lax.all_gather(x_rows, 'dp', axis=1, tiled=True)  69.1 us
    unnamed x25, local copies, waits for them, and re-layouts  14.6 us
    all_to_all x1, blocking collectives, body(): lax.all_to_all(x_part, 'hst', split_axis=0, concat_axis=2, tiled=True)  10.6 us
  transfers between devices with their start and end apart: 5, of which 5 were waited for; matrix products, arithmetic and copies ran while one was open for 4% of the time, Pallas kernels for 0%

commit v1 on v0

v1 whole, which is shorter than its diff:
```python
import jax
import jax.numpy as jnp
from jax import lax
from jax.experimental import pallas as pl
from jax.experimental.pallas import tpu as pltpu
from jax.sharding import PartitionSpec as P

F32, BF16 = jnp.float32, jnp.bfloat16
HIGHEST = lax.Precision.HIGHEST
MESH = pl.DeviceIdType.MESH
NX, NZ, HOSTS, CAP, TOK = 4, 8, 8, 4, 16
ROWS = NX * CAP
R = NZ * ROWS
FEAT = 896
QL = 2 * FEAT
D = NX * QL
FF = 152
LA = 768
TILES = FEAT // 128
MSGS = 192
PLACE = {0: 0, 1: 1, 7: 2, 2: 3, 6: 4, 3: 5, 5: 6, 4: 7}
CHUNKS = ((0, 16), (16, 32), (48, 32), (80, 48))


def rows(k):
    return pl.ds(ROWS * PLACE[k % NZ], ROWS)


def iota(shape, dim):
    return lax.broadcasted_iota(jnp.int32, shape, dim)


def mm(a, b, ca, cb, precision=None):
    return lax.dot_general(
        a, b, (((ca,), (cb,)), ((), ())), precision=precision, preferred_element_type=F32
    )


def add(total, part):
    total[...] = (total[...].astype(F32) + part[...].astype(F32)).astype(BF16)


class Links:
    def __init__(self, ssem, rsem):
        self.ssem, self.rsem, self.sent = ssem, rsem, []

    def send(self, src, dst, land, dev):
        i = len(self.sent)
        copy = pltpu.make_async_remote_copy(
            src_ref=src, dst_ref=dst, send_sem=self.ssem.at[i], recv_sem=self.rsem.at[i],
            device_id=dev, device_id_type=MESH,
        )
        copy.start()
        self.sent.append(copy)
        return pltpu.make_async_remote_copy(
            src_ref=land, dst_ref=land, send_sem=self.ssem.at[i], recv_sem=self.rsem.at[i],
            device_id=dev, device_id_type=MESH,
        ).wait_recv


def ring_steps(*gens):
    for g in gens:
        next(g, None)


def gather(G, links, place):
    x, xp, xm, xo, dxp, dxm, dzp, dzm = place

    def along_x(rs, lo, hi):
        mid = (lo + hi) // 2
        a, b = pl.ds(lo, mid - lo), pl.ds(mid, hi - mid)
        full = pl.ds(lo, hi - lo)
        mine = G.at[x, rs, full]
        p = links.send(mine, mine, G.at[xm, rs, full], dxp)
        m = links.send(mine, mine, G.at[xp, rs, full], dxm)
        yield
        p()
        f = links.send(G.at[xm, rs, a], G.at[xm, rs, a], G.at[xo, rs, a], dxp)
        m()
        g = links.send(G.at[xp, rs, b], G.at[xp, rs, b], G.at[xo, rs, b], dxm)
        yield
        f()
        g()

    def along_z(q, lo, hi):
        mid = (lo + hi) // 2
        p = m = None
        for s in range(1, NZ // 2 + 1):
            if s > 1:
                p()
            lu = pl.ds(lo, hi - lo) if s < NZ // 2 else pl.ds(lo, mid - lo)
            ld = pl.ds(lo, hi - lo) if s < NZ // 2 else pl.ds(mid, hi - mid)
            there = G.at[q, rows(-s), lu]
            p = links.send(G.at[q, rows(1 - s), lu], there, there, dzp)
            if s > 1:
                m()
            there = G.at[q, rows(s), ld]
            m = links.send(G.at[q, rows(s - 1), ld], there, there, dzm)
            yield
        p()
        m()

    a1 = along_x(rows(0), 0, LA)
    b1 = along_z(x, LA, QL)
    b2 = [along_x(pl.ds(lo, n), LA, QL) for lo, n in CHUNKS]
    a2 = [along_z(pl.ds(2 * i, 2), 0, LA) for i in range(2)]
    ring_steps(a1, b1, b2[0])
    yield
    ring_steps(a1, b1, b2[1])
    yield
    ring_steps(a1, a2[0], a2[1])
    yield
    ring_steps(b2[0], b1, b2[2])
    yield
    ring_steps(a2[0], a2[1])
    yield
    ring_steps(b2[1], b1)
    yield
    ring_steps(a2[0], a2[1])
    yield
    ring_steps(b1, b2[3], b2[2])
    yield
    ring_steps(a2[0], a2[1])
    yield
    ring_steps(b2[3])
    yield
    ring_steps(*b2, *a2)


def scatter(O, landing, links, place):
    x, xp, xm, xo, dxp, dxm, dzp, dzm = place
    za, zb, xa1, xa2, xb1, xb2 = landing

    def along_x(rs, lrs, lo, hi, half, whole):
        mid = (lo + hi) // 2
        n = mid - lo
        a, b = pl.ds(lo, n), pl.ds(mid, n)
        full = pl.ds(lo, hi - lo)
        ha, hb = half.at[0, lrs], half.at[1, lrs]
        wa, wb = whole.at[0, lrs], whole.at[1, lrs]
        p = links.send(O.at[xo, rs, a], ha, ha, dxp)
        m = links.send(O.at[xo, rs, b], hb, hb, dxm)
        yield
        p()
        add(O.at[xp, rs, a], ha)
        p = links.send(O.at[xp, rs, full], wa, wa, dxp)
        m()
        add(O.at[xm, rs, b], hb)
        m = links.send(O.at[xm, rs, full], wb, wb, dxm)
        yield
        p()
        add(O.at[x, rs, full], wa)
        m()
        add(O.at[x, rs, full], wb)

    def along_z(q, lq, lo, hi, land):
        mid = (lo + hi) // 2
        n = mid - lo
        a, b = pl.ds(lo, n), pl.ds(mid, n)
        full = pl.ds(lo, hi - lo)

        def at(d, s):
            ref = land.at[d, s] if lq is None else land.at[d, s, lq]
            if s:
                return ref
            return ref.at[:, pl.ds(0, n)] if lq is None else ref.at[:, :, pl.ds(0, n)]

        far = NZ // 2
        m = links.send(O.at[q, rows(far), a], at(0, 0), at(0, 0), dzm)
        p = links.send(O.at[q, rows(far), b], at(1, 0), at(1, 0), dzp)
        yield
        for s in range(1, far):
            k = far - s
            m()
            add(O.at[q, rows(-k), a if s == 1 else full], at(0, s - 1))
            m = links.send(O.at[q, rows(-k), full], at(0, s), at(0, s), dzm)
            p()
            add(O.at[q, rows(k), b if s == 1 else full], at(1, s - 1))
            p = links.send(O.at[q, rows(k), full], at(1, s), at(1, s), dzp)
            yield
        m()
        add(O.at[q, rows(0), full], at(0, far - 1))
        p()
        add(O.at[q, rows(0), full], at(1, far - 1))

    az = [along_z(pl.ds(2 * i, 2), pl.ds(2 * i, 2), 0, LA, za) for i in range(2)]
    bx = [along_x(pl.ds(lo, n), pl.ds(lo, n), LA, QL, xb1, xb2) for lo, n in CHUNKS]
    bz = along_z(x, None, LA, QL, zb)
    ax = along_x(rows(0), slice(None), 0, LA, xa1, xa2)
    ring_steps(*az, bx[3], bx[2])
    yield
    ring_steps(bx[3], bx[1])
    yield
    ring_steps(*az, bx[2], bx[0])
    yield
    ring_steps(bx[3], bz, bx[1])
    yield
    ring_steps(*az)
    yield
    ring_steps(bx[2], bz, bx[0])
    yield
    ring_steps(*az)
    yield
    ring_steps(bx[1], bz)
    yield
    ring_steps(*az, ax)
    yield
    ring_steps(bz, ax, bx[0])
    yield
    ring_steps(bz, ax)


def kernel(
    tok_ref, cot_ref, ids_ref, gate_ref, wg_hbm, wu_hbm, wd_hbm,
    mixed_ref, gtok_ref, gg_hbm, gu_hbm, gd_hbm,
    wg, wu, wd, gx, gd, oo, ob, accg, accu, accd, act_s, dg_s, du_s, grad, qt, qw,
    msend, mrecv, rsend, rrecv, *rest,
):
    land_o, land_b = rest[0:6], rest[6:12]
    wsem, gsem, ssem, rsem, asend, arecv = rest[12:]
    dp, h = lax.axis_index("dp"), lax.axis_index("hst")
    z, x = dp // NX, dp % NX
    xp, xm, xo = (x + 1) % NX, (x + NX - 1) % NX, (x + 2) % NX
    dev = lambda zz, xx, hh: (zz * NX + xx, hh)
    dxp, dxm = dev(z, xp, h), dev(z, xm, h)
    dzp, dzm = dev((z + 1) % NZ, x, h), dev((z + NZ - 1) % NZ, x, h)
    place = (x, xp, xm, xo, dxp, dxm, dzp, dzm)
    hq, hr = h // 2, h % 2
    other = x != hq

    loads = [
        pltpu.make_async_copy(src.at[0], dst, wsem.at[i])
        for i, (src, dst) in enumerate(((wg_hbm, wg), (wu_hbm, wu), (wd_hbm, wd)))
    ]
    for load in loads:
        load.start()

    barrier = pltpu.get_barrier_semaphore()

    def greet(device):
        pl.semaphore_signal(barrier, inc=1, device_id=device, device_id_type=MESH)

    turn = (hq - x + NX) % NX
    greet(dzp)
    greet(dzm)
    for k in range(1, HOSTS):
        greet(dev(z, hq, (h + k) % HOSTS))
    for i in range(1, NX):
        for r in range(2):
            greet(dev(z, (hq + i) % NX, 2 * x + r))

    @pl.when(other)
    def _():
        greet(dev(z, hq, h))

        @pl.when(hq != xp)
        def _():
            greet(dxp)

        @pl.when(hq != xm)
        def _():
            greet(dxm)

    ids, gates = ids_ref[...], gate_ref[...]
    lane = iota((TOK, HOSTS * CAP), 1)
    expert, slot = lane // CAP, (lane % CAP).astype(F32)
    hit0 = (ids[:, 0:1] == expert).astype(F32)
    hit1 = (ids[:, 1:2] == expert).astype(F32)
    below = (iota((TOK, TOK), 0) > iota((TOK, TOK), 1)).astype(BF16)
    before = mm(below, (hit0 + hit1).astype(BF16), 1, 0)
    hit0 = jnp.where(before == slot, hit0, 0.0)
    hit1 = jnp.where(before + (ids[:, 0:1] == expert).astype(F32) == slot, hit1, 0.0)
    wide = (HOSTS * CAP, HOSTS * 32)
    spread = (
        (iota(wide, 0) // CAP == iota(wide, 1) // 32)
        & (iota(wide, 0) % CAP == iota(wide, 1) % CAP)
    ).astype(F32)
    sel = mm(hit0 + hit1, spread, 1, 0, HIGHEST)
    wei = mm(hit0 * gates[:, 0:1] + hit1 * gates[:, 1:2], spread, 1, 0, HIGHEST)
    big = (8 * TOK, HOSTS * 32)
    tile = iota(big, 0) // TOK
    same = (tile == (iota(big, 1) // CAP) % 8) & (tile < TILES)
    qt[...] = jnp.where(same, jnp.concatenate([sel] * 8, axis=0), 0.0)
    qw[...] = jnp.where(same, jnp.concatenate([wei] * 8, axis=0), 0.0)

    def stacked(ref):
        parts = [ref[:, 128 * j : 128 * j + 128] for j in range(TILES)]
        return jnp.concatenate(parts + [jnp.zeros((TOK, 128), ref.dtype)], axis=0)

    xm_rows = mm(qt[...].astype(BF16), stacked(tok_ref), 0, 0).astype(BF16)
    msend[0] = xm_rows.reshape(HOSTS, 32, 128)
    dm_rows = mm(qw[...], stacked(cot_ref).astype(F32), 0, 0, HIGHEST).astype(BF16)
    msend[1] = dm_rows.reshape(HOSTS, 32, 128)

    sq = (128, 128)
    bi, mi = iota(sq, 0), iota(sq, 1)

    def matches(blk, msg):
        return (
            (blk // 16 == (msg // 4) % 8)
            & ((blk // 4) % 4 == msg // 32)
            & (blk % 4 == msg % 4)
        ).astype(F32).astype(BF16)

    into_block, into_msg = matches(bi, mi), matches(mi, bi)

    pl.semaphore_wait(barrier, 18 - 3 * ((NX - turn) // NX) - turn % 2)

    def exchange_out(which):
        copies = []
        for k in range(HOSTS):
            e = (h + k) % HOSTS
            copy = pltpu.make_async_remote_copy(
                src_ref=msend.at[which, e], dst_ref=mrecv.at[which, hr, x],
                send_sem=asend.at[which, k], recv_sem=arecv.at[which, hr * NX + x],
                device_id=dev(z, hq, e), device_id_type=MESH,
            )
            if k:
                copy.start()
            else:
                pl.when(other)(copy.start)
            copies.append(copy)

        @pl.when(jnp.logical_not(other))
        def _():
            mrecv[which, hr, x] = msend[which, h]

        return copies

    def exchange_in(which, block):
        for i in range(NX):
            for r in range(2):
                xi = (x + i) % NX
                land = mrecv.at[which, r, xi]
                copy = pltpu.make_async_remote_copy(
                    src_ref=land, dst_ref=land,
                    send_sem=asend.at[which, 0], recv_sem=arecv.at[which, r * NX + xi],
                    device_id=dev(z, xi, 2 * x + r), device_id_type=MESH,
                )
                if i:
                    copy.wait_recv()
                else:
                    pl.when(2 * x + r != h)(copy.wait_recv)
        for r in range(2):
            got = mm(into_block, mrecv[which, r].reshape(128, 128), 1, 0).astype(BF16)
            for j in range(TILES):
                lo = r * FEAT + 128 * j
                block[x, 0:ROWS, lo : lo + 128] = got[16 * j : 16 * j + 16]

    def return_out(which, block):
        copies = []
        for r in range(2):
            parts = [
                block[x, 0:ROWS, r * FEAT + 128 * j : r * FEAT + 128 * j + 128]
                for j in range(TILES)
            ]
            parts.append(jnp.zeros((ROWS, 128), BF16))
            got = mm(into_msg, jnp.concatenate(parts, axis=0), 1, 0).astype(BF16)
            rsend[which, r] = got.reshape(NX, 32, 128)
        for i in range(NX):
            for r in range(2):
                xi = (x + i) % NX
                copy = pltpu.make_async_remote_copy(
                    src_ref=rsend.at[which, r, xi], dst_ref=rrecv.at[which, h],
                    send_sem=asend.at[2 + which, 2 * i + r], recv_sem=arecv.at[2 + which, h],
                    device_id=dev(z, xi, 2 * x + r), device_id_type=MESH,
                )
                if i:
                    copy.start()
                else:
                    pl.when(2 * x + r != h)(copy.start)
                copies.append(copy)

        @pl.when(jnp.logical_not(other))
        def _():
            rrecv[which, h] = rsend[which, hr, x]

        return copies

    def return_in(which, table, out):
        for k in range(HOSTS):
            e = (h + k) % HOSTS
            land = rrecv.at[which, e]
            copy = pltpu.make_async_remote_copy(
                src_ref=land, dst_ref=land,
                send_sem=asend.at[2 + which, 0], recv_sem=arecv.at[2 + which, e],
                device_id=dev(z, hq, e), device_id_type=MESH,
            )
            if k:
                copy.wait_recv()
            else:
                pl.when(other)(copy.wait_recv)
        got = rrecv[which].reshape(HOSTS * 32, 128).astype(F32)
        res = mm(table[...], got, 1, 0, HIGHEST).astype(BF16)
        for j in range(TILES):
            out[:, 128 * j : 128 * j + 128] = res[16 * j : 16 * j + 16]

    links = Links(ssem, rsem)
    quarter = lambda q: slice(q * QL, (q + 1) * QL)

    def gate_task(q):
        g = mm(gx[q], wg[:, quarter(q)], 1, 1)
        u = mm(gx[q], wu[:, quarter(q)], 1, 1)
        accg[...] = g if q == 0 else accg[...] + g
        accu[...] = u if q == 0 else accu[...] + u

    def act_task():
        g = accg[...]
        act_s[...] = (g * jax.nn.sigmoid(g) * accu[...]).astype(BF16)

    def out_task(q):
        oo[q] = mm(act_s[...], wd[:, quarter(q)], 1, 0).astype(BF16)

    def da_task(q):
        a = mm(gd[q], wd[:, quarter(q)], 1, 1)
        accd[...] = a if q == 0 else accd[...] + a

    def hidden_task():
        g, u, a = accg[...], accu[...], accd[...]
        s = jax.nn.sigmoid(g)
        dg_s[...] = (a * u * s * (1.0 + g * (1.0 - s))).astype(BF16)
        du_s[...] = (a * g * s).astype(BF16)

    def back_task(q):
        part = mm(dg_s[...], wg[:, quarter(q)], 1, 0) + mm(du_s[...], wu[:, quarter(q)], 1, 0)
        ob[q] = part.astype(BF16)

    stores = []

    def grad_task(i, q):
        left, right, out = ((dg_s, gx, gg_hbm), (du_s, gx, gu_hbm), (act_s, gd, gd_hbm))[i]
        grad[i, :, quarter(q)] = mm(left[...], right[q], 0, 0).astype(BF16)
        if q == NX - 1:
            store = pltpu.make_async_copy(grad.at[i], out.at[0], gsem.at[i])
            store.start()
            stores.append(store)

    def task(f, *args):
        return lambda: f(*args)

    def drive(gen, tasks, per=1):
        tasks = list(tasks)
        for _ in gen:
            for t in tasks[:per]:
                t()
            tasks = tasks[per:]
        for t in tasks:
            t()

    quarters = range(NX)
    pending = exchange_out(0) + exchange_out(1)
    exchange_in(0, gx)
    run = gather(gx, links, place)
    next(run)
    exchange_in(1, gd)
    run_d = gather(gd, links, place)
    for step, _ in enumerate(run):
        if step == 8:
            next(run_d)
    loads[0].wait()
    loads[1].wait()
    loads[2].wait()
    tasks = [task(gate_task, q) for q in quarters] + [act_task]
    tasks += [task(out_task, q) for q in quarters]
    drive(run_d, tasks)
    run = scatter(oo, land_o, links, place)
    tasks = [task(da_task, q) for q in quarters] + [hidden_task]
    tasks += [task(back_task, q) for q in quarters]
    drive(run, tasks)
    run = scatter(ob, land_b, links, place)
    next(run)
    pending += return_out(0, oo)
    tasks = [task(grad_task, i, q) for i in range(3) for q in quarters]
    drive(run, tasks, 2)
    pending += return_out(1, ob)
    return_in(0, qw, mixed_ref)
    return_in(1, qt, gtok_ref)

    for store in stores:
        store.wait()
    for copy in links.sent:
        copy.wait_send()
    for n, copy in enumerate(pending):
        first = n < 2 * HOSTS
        if first and n % HOSTS == 0:
            pl.when(other)(copy.wait_send)
        elif not first and n % HOSTS < 2:
            pl.when(2 * x + n % HOSTS != h)(copy.wait_send)
        else:
            copy.wait_send()


def body(tokens, cotangent, expert_ids, gate_values, w_gate, w_up, w_down):
    vmem, hbm = pl.BlockSpec(memory_space=pltpu.VMEM), pl.BlockSpec(memory_space=pl.ANY)
    rows_out = jax.ShapeDtypeStruct((TOK, FEAT), BF16)
    grad_out = jax.ShapeDtypeStruct((1, FF, D), BF16)
    landing = [
        pltpu.VMEM((2, 4, NX, ROWS, LA), BF16),
        pltpu.VMEM((2, 4, ROWS, QL - LA), BF16),
        pltpu.VMEM((2, ROWS, LA // 2), BF16),
        pltpu.VMEM((2, ROWS, LA), BF16),
        pltpu.VMEM((2, R, (QL - LA) // 2), BF16),
        pltpu.VMEM((2, R, QL - LA), BF16),
    ]
    weight, table = pltpu.VMEM((FF, D), BF16), pltpu.VMEM((NX, R, QL), BF16)
    acc, hid = pltpu.VMEM((R, FF), F32), pltpu.VMEM((R, FF), BF16)
    message = pltpu.VMEM((2, HOSTS, 32, 128), BF16)
    blocks = pltpu.VMEM((2, 2, NX, 32, 128), BF16)
    return pl.pallas_call(
        kernel,
        out_shape=(rows_out, rows_out, grad_out, grad_out, grad_out),
        in_specs=[vmem] * 4 + [hbm] * 3,
        out_specs=(vmem, vmem, hbm, hbm, hbm),
        scratch_shapes=[
            weight, weight, weight, table, table, table, table, acc, acc, acc, hid, hid, hid,
            pltpu.VMEM((3, FF, D), BF16),
            pltpu.VMEM((8 * TOK, HOSTS * 32), F32), pltpu.VMEM((8 * TOK, HOSTS * 32), F32),
            message, blocks, blocks, message,
            *landing, *landing,
            pltpu.SemaphoreType.DMA((3,)), pltpu.SemaphoreType.DMA((3,)),
            pltpu.SemaphoreType.DMA((MSGS,)), pltpu.SemaphoreType.DMA((MSGS,)),
            pltpu.SemaphoreType.DMA((4, 8)), pltpu.SemaphoreType.DMA((4, 8)),
        ],
        compiler_params=pltpu.CompilerParams(
            collective_id=0, has_side_effects=True, vmem_limit_bytes=56 * 1024 * 1024
        ),
    )(tokens, cotangent, expert_ids, gate_values, w_gate, w_up, w_down)


def solution(mesh):
    return jax.shard_map(
        body,
        mesh=mesh,
        in_specs=(
            P("dp", "hst"),
            P("dp", "hst"),
            P("dp", None),
            P("dp", None),
            P("hst", "dp", None),
            P("hst", "dp", None),
            P("hst", "dp", None),
        ),
        out_specs=(
            P("dp", "hst"),
            P("dp", "hst"),
            P("hst", "dp", None),
            P("hst", "dp", None),
            P("hst", "dp", None),
        ),
        check_vma=False,
    )
```

time: 433 us -> 131 us (0.30)
  waiting for transfers between devices: 357 us -> 0 us
  Pallas kernels: 0 us -> 117 us
  matrix products: 21.7 us -> 0 us
  blocking collectives: 18.5 us -> 0 us
  between operations: 14.6 us -> 0.64 us
    unnamed x8 -> x0, waiting for transfers between devices: 213 us -> none
    all_gather x2 -> x0, waiting for transfers between devices: 144 us -> none  [the longest x1 75 us: body(): lax.all_gather(d_rows, 'dp', axis=1, tiled=True)]
    pallas_call x0 -> x1, Pallas kernels: none -> 117 us  [body(): pl.pallas_call(kernel, out_shape=(rows_out, rows_out, grad_out, grad_out,...]
    dot_general x13 -> x0, matrix products: 21.7 us -> none  [the longest x1 3.7 us: body(): jnp.einsum('erf,erd->efd', d_gate, x_all, preferred_element_type=jnp.floa...]
    all_to_all x2 -> x0, blocking collectives: 18.5 us -> none  [the longest x1 10.6 us: body(): lax.all_to_all(x_part, 'hst', split_axis=0, concat_axis=2, tiled=True)]
    unnamed x25 -> x11, local copies, waits for them, and re-layouts: 14.6 us -> 12.4 us
  transfers between devices with their start and end apart: 5 -> 0, of which waited for: 5 -> 0; matrix products, arithmetic and copies ran while one was open for 4% -> 0% of each run, Pallas kernels for 0% -> 0%
where the time goes in v1:
time: 131 us; the launch traced here: 130 us
  Pallas kernels  117 us (89%)
  local copies, waits for them, and re-layouts  12.4 us (9%)
    pallas_call x1, Pallas kernels, body(): pl.pallas_call(kernel, out_shape=(rows_out, rows_out, grad_out, grad_out,...  117 us
    unnamed x11, local copies, waits for them, and re-layouts  12.4 us

profile of v1, /device:TPU:1, one launch (start us, length us, event | category | flops | bytes accessed | tf_op | source)
XLA Modules:
  0.0 130.4 jit_solution(14684505104741608154)
XLA Ops:
  0.6 1.4 %copy.12.ids_ref = s32[16,2]{1,0:T(8,128)} copy(s32[16,2]{0,1:T(2,128)} %param.9) | data formatting | bytes 256 | tf_op args[2]
  2.0 1.4 %copy.13.gate_ref = f32[16,2]{1,0:T(8,128)} copy(f32[16,2]{0,1:T(2,128)} %param.10) | data formatting | bytes 256 | tf_op args[3]
  3.3 117.3 %shard_map.110 = (bf16[16,896]{1,0:T(8,128)(2,1)}, bf16[16,896]{1,0:T(8,128)(2,1)}, bf16[1,152,7168]{2,1,0:T(8,128)(2,1)}, bf16[1,152,7168]{2,1,0:T(8,128)(2,1)}, bf16[1,152,7168]{2,1,0:T(8,128)(2,1)}) custom-call(bf16[16,896]{1,0:T(8,128)(2,1)} %tok_ref.1, bf16[16,896]{1,0:T(8,128)(2,1)} %cot_ref.1, s32[16,2]{1,0:T(8,128)} %copy.12.ids_ref, ...), custom_call_target="tpu_custom_call" | custom-call | tf_op jit(solution)/shard_map/pallas_call | solution.py:509
  120.6 1.4 %copy.19 = bf16[16,896]{1,0:T(8,128)(2,1)} copy(bf16[16,896]{1,0:T(8,128)(2,1)} %get-tuple-element.10) | data formatting | bytes 57344
  122.0 1.4 %copy.20 = bf16[16,896]{1,0:T(8,128)(2,1)} copy(bf16[16,896]{1,0:T(8,128)(2,1)} %get-tuple-element.11) | data formatting | bytes 57344
  123.4 0.0 copy-start.1
  123.4 3.2 %copy.21 = bf16[1,152,7168]{2,1,0:T(8,128)(2,1)} copy(bf16[1,152,7168]{2,1,0:T(8,128)(2,1)} %get-tuple-element.12) | data formatting | bytes 4358144
  126.6 0.0 copy-done.1
  126.6 0.0 copy-start
  126.6 1.3 %copy.22 = bf16[1,152,7168]{2,1,0:T(8,128)(2,1)} copy(bf16[1,152,7168]{2,1,0:T(8,128)(2,1)S(1)} %copy-done.1) | data formatting | bytes 4358144
  128.0 1.1 copy-done
  129.0 1.3 %copy.23 = bf16[1,152,7168]{2,1,0:T(8,128)(2,1)} copy(bf16[1,152,7168]{2,1,0:T(8,128)(2,1)S(1)} %copy-done) | data formatting | bytes 4358144
Async XLA Ops:
  123.4 3.3 %copy-start.1 = (bf16[1,152,7168]{2,1,0:T(8,128)(2,1)S(1)}, bf16[1,152,7168]{2,1,0:T(8,128)(2,1)}, u32[]{:S(2)}) copy-start(bf16[1,152,7168]{2,1,0:T(8,128)(2,1)} %get-tuple-element.13) | copy-start | bytes 6537220
  126.6 2.4 %copy-start = (bf16[1,152,7168]{2,1,0:T(8,128)(2,1)S(1)}, bf16[1,152,7168]{2,1,0:T(8,128)(2,1)}, u32[]{:S(2)}) copy-start(bf16[1,152,7168]{2,1,0:T(8,128)(2,1)} %get-tuple-element.14) | copy-start | bytes 6537220

commit v2 on v1

--- a/solution.py
+++ b/solution.py
@@ -19,7 +19,7 @@
 TILES = FEAT // 128
 MSGS = 192
 PLACE = {0: 0, 1: 1, 7: 2, 2: 3, 6: 4, 3: 5, 5: 6, 4: 7}
-CHUNKS = ((0, 16), (16, 32), (48, 32), (80, 48))
+CHUNKS = ((0, 16), (16, 32), (48, 32), (80, 32), (112, 16))
 
 
 def rows(k):
@@ -38,6 +38,11 @@
 
 def add(total, part):
     total[...] = (total[...].astype(F32) + part[...].astype(F32)).astype(BF16)
+
+
+def add2(total, one, two):
+    parts = one[...].astype(F32) + two[...].astype(F32)
+    total[...] = (total[...].astype(F32) + parts).astype(BF16)
 
 
 class Links:
@@ -64,7 +69,18 @@
 
 
 def gather(G, links, place):
-    x, xp, xm, xo, dxp, dxm, dzp, dzm = place
+    x, xp, xm, xo, dxp, dxm, dxo, dzp, dzm = place
+
+    def straight(rs, lo, hi):
+        lanes = pl.ds(lo, hi - lo)
+        mine = G.at[x, rs, lanes]
+        waits = [
+            links.send(mine, mine, G.at[q, rs, lanes], dev)
+            for q, dev in ((xm, dxp), (xp, dxm), (xo, dxo))
+        ]
+        yield
+        for wait in waits:
+            wait()
 
     def along_x(rs, lo, hi):
         mid = (lo + hi) // 2
@@ -100,44 +116,50 @@
         p()
         m()
 
-    a1 = along_x(rows(0), 0, LA)
+    a1 = straight(rows(0), 0, LA)
     b1 = along_z(x, LA, QL)
-    b2 = [along_x(pl.ds(lo, n), LA, QL) for lo, n in CHUNKS]
+    b2 = [along_x(pl.ds(lo, n), LA, QL) for lo, n in CHUNKS[:-1]]
+    b2.append(straight(pl.ds(*CHUNKS[-1]), LA, QL))
     a2 = [along_z(pl.ds(2 * i, 2), 0, LA) for i in range(2)]
     ring_steps(a1, b1, b2[0])
     yield
-    ring_steps(a1, b1, b2[1])
-    yield
-    ring_steps(a1, a2[0], a2[1])
-    yield
-    ring_steps(b2[0], b1, b2[2])
-    yield
-    ring_steps(a2[0], a2[1])
-    yield
-    ring_steps(b2[1], b1)
-    yield
-    ring_steps(a2[0], a2[1])
-    yield
-    ring_steps(b1, b2[3], b2[2])
-    yield
-    ring_steps(a2[0], a2[1])
-    yield
-    ring_steps(b2[3])
-    yield
-    ring_steps(*b2, *a2)
+    ring_steps(a1, *a2, b1, b2[1])
+    yield
+    ring_steps(b2[0], *a2, b1, b2[2])
+    yield
+    ring_steps(b2[1], *a2, b1, b2[3])
+    yield
+    ring_steps(b2[2], *a2, b1, b2[4])
+    yield
+    ring_steps(b2[3], *a2)
+    yield
+    ring_steps(*b2)
 
 
 def scatter(O, landing, links, place):
-    x, xp, xm, xo, dxp, dxm, dzp, dzm = place
-    za, zb, xa1, xa2, xb1, xb2 = landing
-
-    def along_x(rs, lrs, lo, hi, half, whole):
+    x, xp, xm, xo, dxp, dxm, dxo, dzp, dzm = place
+    za, zb, xa, xb, xb1, xb2 = landing
+
+    def straight(rs, lo, hi, land):
+        lanes = pl.ds(lo, hi - lo)
+        waits = [
+            links.send(O.at[q, rs, lanes], land.at[i], land.at[i], dev)
+            for i, (q, dev) in enumerate(((xp, dxp), (xm, dxm), (xo, dxo)))
+        ]
+        yield
+        for wait in waits:
+            wait()
+        total = O.at[x, rs, lanes]
+        parts = [land[i].astype(F32) for i in range(3)]
+        total[...] = (total[...].astype(F32) + (parts[0] + parts[1] + parts[2])).astype(BF16)
+
+    def along_x(rs, lo, hi):
         mid = (lo + hi) // 2
         n = mid - lo
         a, b = pl.ds(lo, n), pl.ds(mid, n)
         full = pl.ds(lo, hi - lo)
-        ha, hb = half.at[0, lrs], half.at[1, lrs]
-        wa, wb = whole.at[0, lrs], whole.at[1, lrs]
+        ha, hb = xb1.at[0, rs], xb1.at[1, rs]
+        wa, wb = xb2.at[0, rs], xb2.at[1, rs]
         p = links.send(O.at[xo, rs, a], ha, ha, dxp)
         m = links.send(O.at[xo, rs, b], hb, hb, dxm)
         yield
@@ -149,9 +171,8 @@
         m = links.send(O.at[xm, rs, full], wb, wb, dxm)
         yield
         p()
-        add(O.at[x, rs, full], wa)
         m()
-        add(O.at[x, rs, full], wb)
+        add2(O.at[x, rs, full], wa, wb)
 
     def along_z(q, lq, lo, hi, land):
         mid = (lo + hi) // 2
@@ -179,52 +200,43 @@
             p = links.send(O.at[q, rows(k), full], at(1, s), at(1, s), dzp)
             yield
         m()
-        add(O.at[q, rows(0), full], at(0, far - 1))
         p()
-        add(O.at[q, rows(0), full], at(1, far - 1))
+        add2(O.at[q, rows(0), full], at(0, far - 1), at(1, far - 1))
 
     az = [along_z(pl.ds(2 * i, 2), pl.ds(2 * i, 2), 0, LA, za) for i in range(2)]
-    bx = [along_x(pl.ds(lo, n), pl.ds(lo, n), LA, QL, xb1, xb2) for lo, n in CHUNKS]
+    bx = [along_x(pl.ds(lo, n), LA, QL) for lo, n in CHUNKS[:-1]]
+    bx.append(straight(pl.ds(*CHUNKS[-1]), LA, QL, xb))
     bz = along_z(x, None, LA, QL, zb)
-    ax = along_x(rows(0), slice(None), 0, LA, xa1, xa2)
-    ring_steps(*az, bx[3], bx[2])
-    yield
-    ring_steps(bx[3], bx[1])
-    yield
-    ring_steps(*az, bx[2], bx[0])
-    yield
-    ring_steps(bx[3], bz, bx[1])
-    yield
-    ring_steps(*az)
-    yield
-    ring_steps(bx[2], bz, bx[0])
-    yield
-    ring_steps(*az)
-    yield
-    ring_steps(bx[1], bz)
-    yield
-    ring_steps(*az, ax)
-    yield
-    ring_steps(bz, ax, bx[0])
-    yield
-    ring_steps(bz, ax)
+    ax = straight(rows(0), 0, LA, xa)
+    ring_steps(*az, bx[4], bx[3], bx[2])
+    yield
+    ring_steps(bx[4], bz, *az, bx[3], bx[1])
+    yield
+    ring_steps(*az, bx[3], bz, bx[2], bx[0])
+    yield
+    ring_steps(*az, bx[2], bz, bx[1])
+    yield
+    ring_steps(*az, ax, bx[1], bz, bx[0])
+    yield
+    ring_steps(bx[0], bz, ax)
 
 
 def kernel(
     tok_ref, cot_ref, ids_ref, gate_ref, wg_hbm, wu_hbm, wd_hbm,
-    mixed_ref, gtok_ref, gg_hbm, gu_hbm, gd_hbm,
-    wg, wu, wd, gx, gd, oo, ob, accg, accu, accd, act_s, dg_s, du_s, grad, qt, qw,
+    mixed_ref, gtok_ref, gg_ref, gu_ref, gd_ref,
+    wg, wu, wd, gx, gd, oo, ob, accg, accu, accd, act_s, dg_s, du_s, qt, qw,
     msend, mrecv, rsend, rrecv, *rest,
 ):
     land_o, land_b = rest[0:6], rest[6:12]
-    wsem, gsem, ssem, rsem, asend, arecv = rest[12:]
+    wsem, ssem, rsem, asend, arecv = rest[12:]
     dp, h = lax.axis_index("dp"), lax.axis_index("hst")
     z, x = dp // NX, dp % NX
     xp, xm, xo = (x + 1) % NX, (x + NX - 1) % NX, (x + 2) % NX
     dev = lambda zz, xx, hh: (zz * NX + xx, hh)
     dxp, dxm = dev(z, xp, h), dev(z, xm, h)
+    dxo = dev(z, xo, h)
     dzp, dzm = dev((z + 1) % NZ, x, h), dev((z + NZ - 1) % NZ, x, h)
-    place = (x, xp, xm, xo, dxp, dxm, dzp, dzm)
+    place = (x, xp, xm, xo, dxp, dxm, dxo, dzp, dzm)
     hq, hr = h // 2, h % 2
     other = x != hq
 
@@ -261,22 +273,32 @@
         def _():
             greet(dxm)
 
-    ids, gates = ids_ref[...], gate_ref[...]
+        @pl.when(hq != xo)
+        def _():
+            greet(dxo)
+
+    eye = iota((TOK, TOK), 0) == iota((TOK, TOK), 1)
+
+    def column(ref, k):
+        return jnp.sum(jnp.where(eye, ref[k : k + 1, :], 0), axis=1, keepdims=True)
+
+    id0, id1 = column(ids_ref, 0), column(ids_ref, 1)
+    gate0, gate1 = column(gate_ref, 0), column(gate_ref, 1)
     lane = iota((TOK, HOSTS * CAP), 1)
     expert, slot = lane // CAP, (lane % CAP).astype(F32)
-    hit0 = (ids[:, 0:1] == expert).astype(F32)
-    hit1 = (ids[:, 1:2] == expert).astype(F32)
+    hit0 = (id0 == expert).astype(F32)
+    hit1 = (id1 == expert).astype(F32)
     below = (iota((TOK, TOK), 0) > iota((TOK, TOK), 1)).astype(BF16)
     before = mm(below, (hit0 + hit1).astype(BF16), 1, 0)
     hit0 = jnp.where(before == slot, hit0, 0.0)
-    hit1 = jnp.where(before + (ids[:, 0:1] == expert).astype(F32) == slot, hit1, 0.0)
+    hit1 = jnp.where(before + (id0 == expert).astype(F32) == slot, hit1, 0.0)
     wide = (HOSTS * CAP, HOSTS * 32)
     spread = (
         (iota(wide, 0) // CAP == iota(wide, 1) // 32)
         & (iota(wide, 0) % CAP == iota(wide, 1) % CAP)
     ).astype(F32)
     sel = mm(hit0 + hit1, spread, 1, 0, HIGHEST)
-    wei = mm(hit0 * gates[:, 0:1] + hit1 * gates[:, 1:2], spread, 1, 0, HIGHEST)
+    wei = mm(hit0 * gate0 + hit1 * gate1, spread, 1, 0, HIGHEST)
     big = (8 * TOK, HOSTS * 32)
     tile = iota(big, 0) // TOK
     same = (tile == (iota(big, 1) // CAP) % 8) & (tile < TILES)
@@ -304,7 +326,7 @@
 
     into_block, into_msg = matches(bi, mi), matches(mi, bi)
 
-    pl.semaphore_wait(barrier, 18 - 3 * ((NX - turn) // NX) - turn % 2)
+    pl.semaphore_wait(barrier, 18 - 3 * ((NX - turn) // NX))
 
     def exchange_out(which):
         copies = []
@@ -425,59 +447,54 @@
         part = mm(dg_s[...], wg[:, quarter(q)], 1, 0) + mm(du_s[...], wu[:, quarter(q)], 1, 0)
         ob[q] = part.astype(BF16)
 
-    stores = []
-
     def grad_task(i, q):
-        left, right, out = ((dg_s, gx, gg_hbm), (du_s, gx, gu_hbm), (act_s, gd, gd_hbm))[i]
-        grad[i, :, quarter(q)] = mm(left[...], right[q], 0, 0).astype(BF16)
-        if q == NX - 1:
-            store = pltpu.make_async_copy(grad.at[i], out.at[0], gsem.at[i])
-            store.start()
-            stores.append(store)
+        left, right, out = ((dg_s, gx, gg_ref), (du_s, gx, gu_ref), (act_s, gd, gd_ref))[i]
+        out[0, :, quarter(q)] = mm(left[...], right[q], 0, 0).astype(BF16)
 
     def task(f, *args):
         return lambda: f(*args)
-
-    def drive(gen, tasks, per=1):
-        tasks = list(tasks)
-        for _ in gen:
-            for t in tasks[:per]:
-                t()
-            tasks = tasks[per:]
-        for t in tasks:
-            t()
 
     quarters = range(NX)
     pending = exchange_out(0) + exchange_out(1)
     exchange_in(0, gx)
-    run = gather(gx, links, place)
-    next(run)
+    run_x = gather(gx, links, place)
+    next(run_x)
     exchange_in(1, gd)
     run_d = gather(gd, links, place)
-    for step, _ in enumerate(run):
-        if step == 8:
-            next(run_d)
-    loads[0].wait()
-    loads[1].wait()
-    loads[2].wait()
-    tasks = [task(gate_task, q) for q in quarters] + [act_task]
-    tasks += [task(out_task, q) for q in quarters]
-    drive(run_d, tasks)
-    run = scatter(oo, land_o, links, place)
-    tasks = [task(da_task, q) for q in quarters] + [hidden_task]
-    tasks += [task(back_task, q) for q in quarters]
-    drive(run, tasks)
-    run = scatter(ob, land_b, links, place)
-    next(run)
+    next(run_d)
+    for load in loads:
+        load.wait()
+    for _ in range(5):
+        ring_steps(run_x, run_d)
+    ring_steps(run_x)
+    for q in quarters:
+        gate_task(q)
+    ring_steps(run_d)
+    act_task()
+    for q in quarters:
+        out_task(q)
+    run_o = scatter(oo, land_o, links, place)
+    next(run_o)
+    for q in quarters:
+        da_task(q)
+    hidden_task()
+    for q in quarters:
+        back_task(q)
+    run_b = scatter(ob, land_b, links, place)
+    next(run_b)
+    tasks = [task(grad_task, i, q) for i in range(3) for q in quarters]
+    for _ in range(4):
+        ring_steps(run_o, run_b)
+        for t in tasks[:3]:
+            t()
+        tasks = tasks[3:]
+    ring_steps(run_o)
     pending += return_out(0, oo)
-    tasks = [task(grad_task, i, q) for i in range(3) for q in quarters]
-    drive(run, tasks, 2)
+    ring_steps(run_b)
     pending += return_out(1, ob)
     return_in(0, qw, mixed_ref)
     return_in(1, qt, gtok_ref)
 
-    for store in stores:
-        store.wait()
     for copy in links.sent:
         copy.wait_send()
     for n, copy in enumerate(pending):
@@ -490,15 +507,23 @@
             copy.wait_send()
 
 
+def write_out(*refs):
+    parts, outs, sem = refs[:5], refs[5:10], refs[10]
+    copies = [pltpu.make_async_copy(parts[i], outs[i], sem.at[i]) for i in range(5)]
+    for copy in copies:
+        copy.start()
+    for copy in copies:
+        copy.wait()
+
+
 def body(tokens, cotangent, expert_ids, gate_values, w_gate, w_up, w_down):
     vmem, hbm = pl.BlockSpec(memory_space=pltpu.VMEM), pl.BlockSpec(memory_space=pl.ANY)
-    rows_out = jax.ShapeDtypeStruct((TOK, FEAT), BF16)
-    grad_out = jax.ShapeDtypeStruct((1, FF, D), BF16)
+    shapes = [(TOK, FEAT)] * 2 + [(1, FF, D)] * 3
     landing = [
         pltpu.VMEM((2, 4, NX, ROWS, LA), BF16),
         pltpu.VMEM((2, 4, ROWS, QL - LA), BF16),
-        pltpu.VMEM((2, ROWS, LA // 2), BF16),
-        pltpu.VMEM((2, ROWS, LA), BF16),
+        pltpu.VMEM((3, ROWS, LA), BF16),
+        pltpu.VMEM((3, ROWS, QL - LA), BF16),
         pltpu.VMEM((2, R, (QL - LA) // 2), BF16),
         pltpu.VMEM((2, R, QL - LA), BF16),
     ]
@@ -506,25 +531,32 @@
     acc, hid = pltpu.VMEM((R, FF), F32), pltpu.VMEM((R, FF), BF16)
     message = pltpu.VMEM((2, HOSTS, 32, 128), BF16)
     blocks = pltpu.VMEM((2, 2, NX, 32, 128), BF16)
-    return pl.pallas_call(
+    parts = pl.pallas_call(
         kernel,
-        out_shape=(rows_out, rows_out, grad_out, grad_out, grad_out),
+        out_shape=[pltpu.VMEM(shape, BF16) for shape in shapes],
         in_specs=[vmem] * 4 + [hbm] * 3,
-        out_specs=(vmem, vmem, hbm, hbm, hbm),
+        out_specs=[vmem] * 5,
         scratch_shapes=[
             weight, weight, weight, table, table, table, table, acc, acc, acc, hid, hid, hid,
-            pltpu.VMEM((3, FF, D), BF16),
             pltpu.VMEM((8 * TOK, HOSTS * 32), F32), pltpu.VMEM((8 * TOK, HOSTS * 32), F32),
             message, blocks, blocks, message,
             *landing, *landing,
-            pltpu.SemaphoreType.DMA((3,)), pltpu.SemaphoreType.DMA((3,)),
+            pltpu.SemaphoreType.DMA((3,)),
             pltpu.SemaphoreType.DMA((MSGS,)), pltpu.SemaphoreType.DMA((MSGS,)),
             pltpu.SemaphoreType.DMA((4, 8)), pltpu.SemaphoreType.DMA((4, 8)),
         ],
         compiler_params=pltpu.CompilerParams(
-            collective_id=0, has_side_effects=True, vmem_limit_bytes=56 * 1024 * 1024
+            collective_id=0, has_side_effects=True, vmem_limit_bytes=52 * 1024 * 1024
         ),
-    )(tokens, cotangent, expert_ids, gate_values, w_gate, w_up, w_down)
+    )(tokens, cotangent, expert_ids.T, gate_values.T, w_gate, w_up, w_down)
+    return pl.pallas_call(
+        write_out,
+        out_shape=[jax.ShapeDtypeStruct(shape, BF16) for shape in shapes],
+        in_specs=[vmem] * 5,
+        out_specs=[hbm] * 5,
+        scratch_shapes=[pltpu.SemaphoreType.DMA((5,))],
+        compiler_params=pltpu.CompilerParams(vmem_limit_bytes=1024 * 1024),
+    )(*[pltpu.with_memory_space_constraint(part, pltpu.VMEM) for part in parts])
 
 
 def solution(mesh):

time: 131 us -> 85.8 us (0.65)
  Pallas kernels: 117 us -> 85 us
  local copies, waits for them, and re-layouts: 12.4 us -> 0 us
    pallas_call x1 -> x2, Pallas kernels: 117 us -> 85 us  [the longest x1 82.2 us: body(): pl.pallas_call(kernel, out_shape=[pltpu.VMEM(shape, BF16) for shape in sh...]
    unnamed x11 -> x0, local copies, waits for them, and re-layouts: 12.4 us -> none
where the time goes in v2:
time: 85.8 us; the launch traced here: 85.7 us
  Pallas kernels  85 us (99%)
    pallas_call x1, Pallas kernels, body(): pl.pallas_call(kernel, out_shape=[pltpu.VMEM(shape, BF16) for shape in sh...  82.2 us
    pallas_call x1, Pallas kernels, body(): pl.pallas_call(write_out, out_shape=[jax.ShapeDtypeStruct(shape, BF16) fo...  2.84 us

profile of v2, /device:TPU:1, one launch (start us, length us, event | category | flops | bytes accessed | tf_op | source)
XLA Modules:
  0.0 85.7 jit_solution(2387496746793895090)
XLA Ops:
  0.6 82.2 %shard_map.110 = (bf16[16,896]{1,0:T(8,128)(2,1)S(1)}, bf16[16,896]{1,0:T(8,128)(2,1)S(1)}, bf16[1,152,7168]{2,1,0:T(8,128)(2,1)S(1)}, bf16[1,152,7168]{2,1,0:T(8,128)(2,1)S(1)}, bf16[1,152,7168]{2,1,0:T(8,128)(2,1)S(1)}) custom-call(bf16[16,896]{1,0:T(8,128)(2,1)} %tok_ref.1, bf16[16,896]{1,0:T(8,128)(2,1)} %cot_ref.1, s32[2,16]{1,0:T(2,128)} %bitcast.2, ...), custom_call_target="tpu_custom_call" | custom-call | tf_op jit(solution)/shard_map/pallas_call | solution.py:534
  82.8 2.8 %shard_map.111 = (bf16[16,896]{1,0:T(8,128)(2,1)}, bf16[16,896]{1,0:T(8,128)(2,1)}, bf16[1,152,7168]{2,1,0:T(8,128)(2,1)}, bf16[1,152,7168]{2,1,0:T(8,128)(2,1)}, bf16[1,152,7168]{2,1,0:T(8,128)(2,1)}) custom-call(bf16[16,896]{1,0:T(8,128)(2,1)S(1)} %get-tuple-element.10.refs_0_, bf16[16,896]{1,0:T(8,128)(2,1)S(1)} %get-tuple-element.11.refs_1_, ...), custom_call_target="tpu_custom_call" | custom-call | tf_op jit(solution)/shard_map/pallas_call | solution.py:552

commit v3 on v2

--- a/solution.py
+++ b/solution.py
@@ -17,7 +17,7 @@
 FF = 152
 LA = 768
 TILES = FEAT // 128
-MSGS = 192
+MSGS = 54
 PLACE = {0: 0, 1: 1, 7: 2, 2: 3, 6: 4, 3: 5, 5: 6, 4: 7}
 CHUNKS = ((0, 16), (16, 32), (48, 32), (80, 32), (112, 16))
 
@@ -46,21 +46,24 @@
 
 
 class Links:
-    def __init__(self, ssem, rsem):
-        self.ssem, self.rsem, self.sent = ssem, rsem, []
-
-    def send(self, src, dst, land, dev):
-        i = len(self.sent)
-        copy = pltpu.make_async_remote_copy(
-            src_ref=src, dst_ref=dst, send_sem=self.ssem.at[i], recv_sem=self.rsem.at[i],
+    def __init__(self, ssem, rsem, first):
+        self.ssem, self.rsem, self.next = ssem, rsem, first
+
+    def copy(self, src, dst, dev, i, group):
+        return pltpu.make_async_remote_copy(
+            src_ref=src, dst_ref=dst, send_sem=self.ssem.at[group], recv_sem=self.rsem.at[i],
             device_id=dev, device_id_type=MESH,
         )
-        copy.start()
-        self.sent.append(copy)
-        return pltpu.make_async_remote_copy(
-            src_ref=land, dst_ref=land, send_sem=self.ssem.at[i], recv_sem=self.rsem.at[i],
-            device_id=dev, device_id_type=MESH,
-        ).wait_recv
+
+    def send(self, src, dst, land, dev, group):
+        i = self.next
+        self.next += 1
+        self.copy(src, dst, dev, i, group).start()
+        return self.copy(land, land, dev, i, group).wait_recv
+
+    def wait_sent(self, table, dev):
+        for group, ref in ((0, table.at[0, pl.ds(0, 112)]), (1, table.at[pl.ds(0, 3)])):
+            self.copy(ref, ref, dev, 0, group).wait_send()
 
 
 def ring_steps(*gens):
@@ -75,7 +78,7 @@
         lanes = pl.ds(lo, hi - lo)
         mine = G.at[x, rs, lanes]
         waits = [
-            links.send(mine, mine, G.at[q, rs, lanes], dev)
+            links.send(mine, mine, G.at[q, rs, lanes], dev, 1)
             for q, dev in ((xm, dxp), (xp, dxm), (xo, dxo))
         ]
         yield
@@ -87,18 +90,18 @@
         a, b = pl.ds(lo, mid - lo), pl.ds(mid, hi - mid)
         full = pl.ds(lo, hi - lo)
         mine = G.at[x, rs, full]
-        p = links.send(mine, mine, G.at[xm, rs, full], dxp)
-        m = links.send(mine, mine, G.at[xp, rs, full], dxm)
+        p = links.send(mine, mine, G.at[xm, rs, full], dxp, 1)
+        m = links.send(mine, mine, G.at[xp, rs, full], dxm, 1)
         yield
         p()
-        f = links.send(G.at[xm, rs, a], G.at[xm, rs, a], G.at[xo, rs, a], dxp)
+        f = links.send(G.at[xm, rs, a], G.at[xm, rs, a], G.at[xo, rs, a], dxp, 1)
         m()
-        g = links.send(G.at[xp, rs, b], G.at[xp, rs, b], G.at[xo, rs, b], dxm)
+        g = links.send(G.at[xp, rs, b], G.at[xp, rs, b], G.at[xo, rs, b], dxm, 1)
         yield
         f()
         g()
 
-    def along_z(q, lo, hi):
+    def along_z(q, lo, hi, group):
         mid = (lo + hi) // 2
         p = m = None
         for s in range(1, NZ // 2 + 1):
@@ -107,33 +110,31 @@
             lu = pl.ds(lo, hi - lo) if s < NZ // 2 else pl.ds(lo, mid - lo)
             ld = pl.ds(lo, hi - lo) if s < NZ // 2 else pl.ds(mid, hi - mid)
             there = G.at[q, rows(-s), lu]
-            p = links.send(G.at[q, rows(1 - s), lu], there, there, dzp)
+            p = links.send(G.at[q, rows(1 - s), lu], there, there, dzp, group)
             if s > 1:
                 m()
             there = G.at[q, rows(s), ld]
-            m = links.send(G.at[q, rows(s - 1), ld], there, there, dzm)
+            m = links.send(G.at[q, rows(s - 1), ld], there, there, dzm, group)
             yield
         p()
         m()
 
+    own = along_z(x, 0, QL, 0)
     a1 = straight(rows(0), 0, LA)
-    b1 = along_z(x, LA, QL)
     b2 = [along_x(pl.ds(lo, n), LA, QL) for lo, n in CHUNKS[:-1]]
     b2.append(straight(pl.ds(*CHUNKS[-1]), LA, QL))
-    a2 = [along_z(pl.ds(2 * i, 2), 0, LA) for i in range(2)]
-    ring_steps(a1, b1, b2[0])
-    yield
-    ring_steps(a1, *a2, b1, b2[1])
-    yield
-    ring_steps(b2[0], *a2, b1, b2[2])
-    yield
-    ring_steps(b2[1], *a2, b1, b2[3])
-    yield
-    ring_steps(b2[2], *a2, b1, b2[4])
-    yield
-    ring_steps(b2[3], *a2)
-    yield
-    ring_steps(*b2)
+    a2 = [along_z(q, 0, LA, 1) for q in (xp, xm, xo)]
+    ring_steps(own, a1, b2[0])
+    yield
+    ring_steps(a1, *a2, own, b2[1], b2[0])
+    yield
+    ring_steps(own, b2[2], b2[1], *a2)
+    yield
+    ring_steps(own, b2[3], b2[2], *a2, b2[0])
+    yield
+    ring_steps(own, b2[4], b2[3], *a2, b2[1])
+    yield
+    ring_steps(*a2, *b2)
 
 
 def scatter(O, landing, links, place):
@@ -143,7 +144,7 @@
     def straight(rs, lo, hi, land):
         lanes = pl.ds(lo, hi - lo)
         waits = [
-            links.send(O.at[q, rs, lanes], land.at[i], land.at[i], dev)
+            links.send(O.at[q, rs, lanes], land.at[i], land.at[i], dev, 0)
             for i, (q, dev) in enumerate(((xp, dxp), (xm, dxm), (xo, dxo)))
         ]
         yield
@@ -160,21 +161,21 @@
         full = pl.ds(lo, hi - lo)
         ha, hb = xb1.at[0, rs], xb1.at[1, rs]
         wa, wb = xb2.at[0, rs], xb2.at[1, rs]
-        p = links.send(O.at[xo, rs, a], ha, ha, dxp)
-        m = links.send(O.at[xo, rs, b], hb, hb, dxm)
+        p = links.send(O.at[xo, rs, a], ha, ha, dxp, 1)
+        m = links.send(O.at[xo, rs, b], hb, hb, dxm, 1)
         yield
         p()
         add(O.at[xp, rs, a], ha)
-        p = links.send(O.at[xp, rs, full], wa, wa, dxp)
+        p = links.send(O.at[xp, rs, full], wa, wa, dxp, 1)
         m()
         add(O.at[xm, rs, b], hb)
-        m = links.send(O.at[xm, rs, full], wb, wb, dxm)
+        m = links.send(O.at[xm, rs, full], wb, wb, dxm, 1)
         yield
         p()
         m()
         add2(O.at[x, rs, full], wa, wb)
 
-    def along_z(q, lq, lo, hi, land):
+    def along_z(q, lq, lo, hi, land, group):
         mid = (lo + hi) // 2
         n = mid - lo
         a, b = pl.ds(lo, n), pl.ds(mid, n)
@@ -187,26 +188,26 @@
             return ref.at[:, pl.ds(0, n)] if lq is None else ref.at[:, :, pl.ds(0, n)]
 
         far = NZ // 2
-        m = links.send(O.at[q, rows(far), a], at(0, 0), at(0, 0), dzm)
-        p = links.send(O.at[q, rows(far), b], at(1, 0), at(1, 0), dzp)
+        m = links.send(O.at[q, rows(far), a], at(0, 0), at(0, 0), dzm, group)
+        p = links.send(O.at[q, rows(far), b], at(1, 0), at(1, 0), dzp, group)
         yield
         for s in range(1, far):
             k = far - s
             m()
             add(O.at[q, rows(-k), a if s == 1 else full], at(0, s - 1))
-            m = links.send(O.at[q, rows(-k), full], at(0, s), at(0, s), dzm)
+            m = links.send(O.at[q, rows(-k), full], at(0, s), at(0, s), dzm, group)
             p()
             add(O.at[q, rows(k), b if s == 1 else full], at(1, s - 1))
-            p = links.send(O.at[q, rows(k), full], at(1, s), at(1, s), dzp)
+            p = links.send(O.at[q, rows(k), full], at(1, s), at(1, s), dzp, group)
             yield
         m()
         p()
         add2(O.at[q, rows(0), full], at(0, far - 1), at(1, far - 1))
 
-    az = [along_z(pl.ds(2 * i, 2), pl.ds(2 * i, 2), 0, LA, za) for i in range(2)]
+    az = [along_z(pl.ds(2 * i, 2), pl.ds(2 * i, 2), 0, LA, za, 1) for i in range(2)]
     bx = [along_x(pl.ds(lo, n), LA, QL) for lo, n in CHUNKS[:-1]]
     bx.append(straight(pl.ds(*CHUNKS[-1]), LA, QL, xb))
-    bz = along_z(x, None, LA, QL, zb)
+    bz = along_z(x, None, LA, QL, zb, 0)
     ax = straight(rows(0), 0, LA, xa)
     ring_steps(*az, bx[4], bx[3], bx[2])
     yield
@@ -222,9 +223,9 @@
 
 
 def kernel(
-    tok_ref, cot_ref, ids_ref, gate_ref, wg_hbm, wu_hbm, wd_hbm,
+    tok_hbm, cot_hbm, ids_hbm, gate_hbm, wg_hbm, wu_hbm, wd_hbm,
     mixed_ref, gtok_ref, gg_ref, gu_ref, gd_ref,
-    wg, wu, wd, gx, gd, oo, ob, accg, accu, accd, act_s, dg_s, du_s, qt, qw,
+    tok_ref, cot_ref, ids_ref, gate_ref, wg, wu, wd, gx, gd, oo, ob, accg, accu, accd, act_s, dg_s, du_s, qt, qw,
     msend, mrecv, rsend, rrecv, *rest,
 ):
     land_o, land_b = rest[0:6], rest[6:12]
@@ -236,13 +237,18 @@
     dxp, dxm = dev(z, xp, h), dev(z, xm, h)
     dxo = dev(z, xo, h)
     dzp, dzm = dev((z + 1) % NZ, x, h), dev((z + NZ - 1) % NZ, x, h)
-    place = (x, xp, xm, xo, dxp, dxm, dxo, dzp, dzm)
     hq, hr = h // 2, h % 2
-    other = x != hq
-
+    own = (x - hq + NX) % NX
+    turned = [(own + i) % NX for i in (0, 1, NX - 1, 2)]
+    place = (*turned, dxp, dxm, dxo, dzp, dzm)
+    other = own != hq
+    owner = lambda e: dev(z, (hq + e // 2) % NX, e)
+    source = lambda xx, r: dev(z, xx, 2 * own + r)
+
+    small = ((ids_hbm, ids_ref), (gate_hbm, gate_ref), (tok_hbm, tok_ref), (cot_hbm, cot_ref))
+    large = ((wg_hbm.at[0], wg), (wu_hbm.at[0], wu), (wd_hbm.at[0], wd))
     loads = [
-        pltpu.make_async_copy(src.at[0], dst, wsem.at[i])
-        for i, (src, dst) in enumerate(((wg_hbm, wg), (wu_hbm, wu), (wd_hbm, wd)))
+        pltpu.make_async_copy(src, dst, wsem.at[i]) for i, (src, dst) in enumerate(small + large)
     ]
     for load in loads:
         load.start()
@@ -252,31 +258,33 @@
     def greet(device):
         pl.semaphore_signal(barrier, inc=1, device_id=device, device_id_type=MESH)
 
-    turn = (hq - x + NX) % NX
+    turn = (hq - own + NX) % NX
     greet(dzp)
     greet(dzm)
     for k in range(1, HOSTS):
-        greet(dev(z, hq, (h + k) % HOSTS))
+        greet(owner((h + k) % HOSTS))
     for i in range(1, NX):
         for r in range(2):
-            greet(dev(z, (hq + i) % NX, 2 * x + r))
+            greet(source((x + i) % NX, r))
 
     @pl.when(other)
     def _():
-        greet(dev(z, hq, h))
-
-        @pl.when(hq != xp)
+        greet(owner(h))
+
+        @pl.when(turn != 1)
         def _():
             greet(dxp)
 
-        @pl.when(hq != xm)
+        @pl.when(turn != 3)
         def _():
             greet(dxm)
 
-        @pl.when(hq != xo)
+        @pl.when(turn != 2)
         def _():
             greet(dxo)
 
+    for load in loads[:4]:
+        load.wait()
     eye = iota((TOK, TOK), 0) == iota((TOK, TOK), 1)
 
     def column(ref, k):
@@ -310,9 +318,9 @@
         return jnp.concatenate(parts + [jnp.zeros((TOK, 128), ref.dtype)], axis=0)
 
     xm_rows = mm(qt[...].astype(BF16), stacked(tok_ref), 0, 0).astype(BF16)
-    msend[0] = xm_rows.reshape(HOSTS, 32, 128)
+    msend[:, 0:32] = xm_rows.reshape(HOSTS, 32, 128)
     dm_rows = mm(qw[...], stacked(cot_ref).astype(F32), 0, 0, HIGHEST).astype(BF16)
-    msend[1] = dm_rows.reshape(HOSTS, 32, 128)
+    msend[:, 32:64] = dm_rows.reshape(HOSTS, 32, 128)
 
     sq = (128, 128)
     bi, mi = iota(sq, 0), iota(sq, 1)
@@ -328,52 +336,50 @@
 
     pl.semaphore_wait(barrier, 18 - 3 * ((NX - turn) // NX))
 
-    def exchange_out(which):
-        copies = []
+    def exchange_out():
         for k in range(HOSTS):
             e = (h + k) % HOSTS
             copy = pltpu.make_async_remote_copy(
-                src_ref=msend.at[which, e], dst_ref=mrecv.at[which, hr, x],
-                send_sem=asend.at[which, k], recv_sem=arecv.at[which, hr * NX + x],
-                device_id=dev(z, hq, e), device_id_type=MESH,
+                src_ref=msend.at[e], dst_ref=mrecv.at[hr, x],
+                send_sem=asend.at[0, min(k, 1)], recv_sem=arecv.at[0, hr * NX + x],
+                device_id=owner(e), device_id_type=MESH,
             )
             if k:
                 copy.start()
             else:
                 pl.when(other)(copy.start)
-            copies.append(copy)
 
         @pl.when(jnp.logical_not(other))
         def _():
-            mrecv[which, hr, x] = msend[which, h]
-
-        return copies
-
-    def exchange_in(which, block):
+            mrecv[hr, x] = msend[h]
+
+    def exchange_in():
         for i in range(NX):
             for r in range(2):
                 xi = (x + i) % NX
-                land = mrecv.at[which, r, xi]
+                land = mrecv.at[r, xi]
                 copy = pltpu.make_async_remote_copy(
                     src_ref=land, dst_ref=land,
-                    send_sem=asend.at[which, 0], recv_sem=arecv.at[which, r * NX + xi],
-                    device_id=dev(z, xi, 2 * x + r), device_id_type=MESH,
+                    send_sem=asend.at[0, 0], recv_sem=arecv.at[0, r * NX + xi],
+                    device_id=source(xi, r), device_id_type=MESH,
                 )
                 if i:
                     copy.wait_recv()
                 else:
-                    pl.when(2 * x + r != h)(copy.wait_recv)
+                    pl.when(2 * own + r != h)(copy.wait_recv)
+
+    def assemble(which, block):
         for r in range(2):
-            got = mm(into_block, mrecv[which, r].reshape(128, 128), 1, 0).astype(BF16)
+            got = mrecv[r, :, 32 * which : 32 * which + 32].reshape(128, 128)
+            got = mm(into_block, got, 1, 0).astype(BF16)
             for j in range(TILES):
                 lo = r * FEAT + 128 * j
-                block[x, 0:ROWS, lo : lo + 128] = got[16 * j : 16 * j + 16]
+                block[own, 0:ROWS, lo : lo + 128] = got[16 * j : 16 * j + 16]
 
     def return_out(which, block):
-        copies = []
         for r in range(2):
             parts = [
-                block[x, 0:ROWS, r * FEAT + 128 * j : r * FEAT + 128 * j + 128]
+                block[own, 0:ROWS, r * FEAT + 128 * j : r * FEAT + 128 * j + 128]
                 for j in range(TILES)
             ]
             parts.append(jnp.zeros((ROWS, 128), BF16))
@@ -384,20 +390,17 @@
                 xi = (x + i) % NX
                 copy = pltpu.make_async_remote_copy(
                     src_ref=rsend.at[which, r, xi], dst_ref=rrecv.at[which, h],
-                    send_sem=asend.at[2 + which, 2 * i + r], recv_sem=arecv.at[2 + which, h],
-                    device_id=dev(z, xi, 2 * x + r), device_id_type=MESH,
+                    send_sem=asend.at[1 + which, 2 if i else r], recv_sem=arecv.at[1 + which, h],
+                    device_id=source(xi, r), device_id_type=MESH,
                 )
                 if i:
                     copy.start()
                 else:
-                    pl.when(2 * x + r != h)(copy.start)
-                copies.append(copy)
+                    pl.when(2 * own + r != h)(copy.start)
 
         @pl.when(jnp.logical_not(other))
         def _():
             rrecv[which, h] = rsend[which, hr, x]
-
-        return copies
 
     def return_in(which, table, out):
         for k in range(HOSTS):
@@ -405,8 +408,8 @@
             land = rrecv.at[which, e]
             copy = pltpu.make_async_remote_copy(
                 src_ref=land, dst_ref=land,
-                send_sem=asend.at[2 + which, 0], recv_sem=arecv.at[2 + which, e],
-                device_id=dev(z, hq, e), device_id_type=MESH,
+                send_sem=asend.at[1 + which, 0], recv_sem=arecv.at[1 + which, e],
+                device_id=owner(e), device_id_type=MESH,
             )
             if k:
                 copy.wait_recv()
@@ -417,7 +420,7 @@
         for j in range(TILES):
             out[:, 128 * j : 128 * j + 128] = res[16 * j : 16 * j + 16]
 
-    links = Links(ssem, rsem)
+    links = [Links(ssem.at[i], rsem, MSGS * (i % 2)) for i in range(4)]
     quarter = lambda q: slice(q * QL, (q + 1) * QL)
 
     def gate_task(q):
@@ -455,32 +458,33 @@
         return lambda: f(*args)
 
     quarters = range(NX)
-    pending = exchange_out(0) + exchange_out(1)
-    exchange_in(0, gx)
-    run_x = gather(gx, links, place)
+    exchange_out()
+    exchange_in()
+    assemble(0, gx)
+    run_x = gather(gx, links[0], place)
     next(run_x)
-    exchange_in(1, gd)
-    run_d = gather(gd, links, place)
+    assemble(1, gd)
+    run_d = gather(gd, links[1], place)
     next(run_d)
-    for load in loads:
+    for load in loads[4:]:
         load.wait()
-    for _ in range(5):
+    for _ in range(4):
         ring_steps(run_x, run_d)
     ring_steps(run_x)
     for q in quarters:
         gate_task(q)
-    ring_steps(run_d)
     act_task()
     for q in quarters:
         out_task(q)
-    run_o = scatter(oo, land_o, links, place)
+    run_o = scatter(oo, land_o, links[3], place)
     next(run_o)
+    ring_steps(run_d)
     for q in quarters:
         da_task(q)
     hidden_task()
     for q in quarters:
         back_task(q)
-    run_b = scatter(ob, land_b, links, place)
+    run_b = scatter(ob, land_b, links[2], place)
     next(run_b)
     tasks = [task(grad_task, i, q) for i in range(3) for q in quarters]
     for _ in range(4):
@@ -489,22 +493,34 @@
             t()
         tasks = tasks[3:]
     ring_steps(run_o)
-    pending += return_out(0, oo)
+    return_out(0, oo)
     ring_steps(run_b)
-    pending += return_out(1, ob)
+    return_out(1, ob)
     return_in(0, qw, mixed_ref)
     return_in(1, qt, gtok_ref)
 
-    for copy in links.sent:
-        copy.wait_send()
-    for n, copy in enumerate(pending):
-        first = n < 2 * HOSTS
-        if first and n % HOSTS == 0:
-            pl.when(other)(copy.wait_send)
-        elif not first and n % HOSTS < 2:
-            pl.when(2 * x + n % HOSTS != h)(copy.wait_send)
-        else:
-            copy.wait_send()
+    for i, table in enumerate((gx, gd, ob, oo)):
+        links[i].wait_sent(table, dzp)
+
+    def wait_sent(ref, sem):
+        pltpu.make_async_remote_copy(
+            src_ref=ref, dst_ref=ref, send_sem=sem, recv_sem=arecv.at[0, 0],
+            device_id=dzp, device_id_type=MESH,
+        ).wait_send()
+
+    wait_sent(msend.at[pl.ds(1, HOSTS - 1)], asend.at[0, 1])
+
+    @pl.when(other)
+    def _():
+        wait_sent(msend.at[0], asend.at[0, 0])
+
+    for which in range(2):
+        wait_sent(rsend.at[which, :, pl.ds(1, NX - 1)], asend.at[1 + which, 2])
+        for r in range(2):
+
+            @pl.when(2 * own + r != h)
+            def _():
+                wait_sent(rsend.at[which, r, 0], asend.at[1 + which, r])
 
 
 def write_out(*refs):
@@ -529,21 +545,22 @@
     ]
     weight, table = pltpu.VMEM((FF, D), BF16), pltpu.VMEM((NX, R, QL), BF16)
     acc, hid = pltpu.VMEM((R, FF), F32), pltpu.VMEM((R, FF), BF16)
-    message = pltpu.VMEM((2, HOSTS, 32, 128), BF16)
-    blocks = pltpu.VMEM((2, 2, NX, 32, 128), BF16)
     parts = pl.pallas_call(
         kernel,
         out_shape=[pltpu.VMEM(shape, BF16) for shape in shapes],
-        in_specs=[vmem] * 4 + [hbm] * 3,
+        in_specs=[hbm] * 7,
         out_specs=[vmem] * 5,
         scratch_shapes=[
+            pltpu.VMEM((TOK, FEAT), BF16), pltpu.VMEM((TOK, FEAT), BF16),
+            pltpu.VMEM((2, TOK), jnp.int32), pltpu.VMEM((2, TOK), F32),
             weight, weight, weight, table, table, table, table, acc, acc, acc, hid, hid, hid,
             pltpu.VMEM((8 * TOK, HOSTS * 32), F32), pltpu.VMEM((8 * TOK, HOSTS * 32), F32),
-            message, blocks, blocks, message,
+            pltpu.VMEM((HOSTS, 64, 128), BF16), pltpu.VMEM((2, NX, 64, 128), BF16),
+            pltpu.VMEM((2, 2, NX, 32, 128), BF16), pltpu.VMEM((2, HOSTS, 32, 128), BF16),
             *landing, *landing,
-            pltpu.SemaphoreType.DMA((3,)),
-            pltpu.SemaphoreType.DMA((MSGS,)), pltpu.SemaphoreType.DMA((MSGS,)),
-            pltpu.SemaphoreType.DMA((4, 8)), pltpu.SemaphoreType.DMA((4, 8)),
+            pltpu.SemaphoreType.DMA((7,)),
+            pltpu.SemaphoreType.DMA((4, 2)), pltpu.SemaphoreType.DMA((2 * MSGS,)),
+            pltpu.SemaphoreType.DMA((3, 3)), pltpu.SemaphoreType.DMA((3, 8)),
         ],
         compiler_params=pltpu.CompilerParams(
             collective_id=0, has_side_effects=True, vmem_limit_bytes=52 * 1024 * 1024

time: 85.8 us -> 78.1 us (0.910)
  Pallas kernels: 85 us -> 77.4 us
    pallas_call x1, Pallas kernels: 82.2 us -> 74.5 us  [body(): pl.pallas_call(kernel, out_shape=[pltpu.VMEM(shape, BF16) for shape in sh...]
where the time goes in v3:
time: 78.1 us; the launch traced here: 78 us
  Pallas kernels  77.4 us (99%)
    pallas_call x1, Pallas kernels, body(): pl.pallas_call(kernel, out_shape=[pltpu.VMEM(shape, BF16) for shape in sh...  74.5 us
    pallas_call x1, Pallas kernels, body(): pl.pallas_call(write_out, out_shape=[jax.ShapeDtypeStruct(shape, BF16) fo...  2.84 us

profile of v3, /device:TPU:1, one launch (start us, length us, event | category | flops | bytes accessed | tf_op | source)
XLA Modules:
  0.0 78.0 jit_solution(18278459538409619789)
XLA Ops:
  0.6 74.5 %shard_map.110 = (bf16[16,896]{1,0:T(8,128)(2,1)S(1)}, bf16[16,896]{1,0:T(8,128)(2,1)S(1)}, bf16[1,152,7168]{2,1,0:T(8,128)(2,1)S(1)}, bf16[1,152,7168]{2,1,0:T(8,128)(2,1)S(1)}, bf16[1,152,7168]{2,1,0:T(8,128)(2,1)S(1)}) custom-call(bf16[16,896]{1,0:T(8,128)(2,1)} %tok_hbm.1, bf16[16,896]{1,0:T(8,128)(2,1)} %cot_hbm.1, s32[2,16]{1,0:T(2,128)} %bitcast.2, ...), custom_call_target="tpu_custom_call" | custom-call | tf_op jit(solution)/shard_map/pallas_call | solution.py:548
  75.2 2.8 %shard_map.111 = (bf16[16,896]{1,0:T(8,128)(2,1)}, bf16[16,896]{1,0:T(8,128)(2,1)}, bf16[1,152,7168]{2,1,0:T(8,128)(2,1)}, bf16[1,152,7168]{2,1,0:T(8,128)(2,1)}, bf16[1,152,7168]{2,1,0:T(8,128)(2,1)}) custom-call(bf16[16,896]{1,0:T(8,128)(2,1)S(1)} %get-tuple-element.10.refs_0_, bf16[16,896]{1,0:T(8,128)(2,1)S(1)} %get-tuple-element.11.refs_1_, ...), custom_call_target="tpu_custom_call" | custom-call | tf_op jit(solution)/shard_map/pallas_call | solution.py:569

commit v4 on v3

--- a/solution.py
+++ b/solution.py
@@ -79,7 +79,7 @@
         mine = G.at[x, rs, lanes]
         waits = [
             links.send(mine, mine, G.at[q, rs, lanes], dev, 1)
-            for q, dev in ((xm, dxp), (xp, dxm), (xo, dxo))
+            for q, dev in ((xo, dxo), (xm, dxp), (xp, dxm))
         ]
         yield
         for wait in waits:
@@ -145,7 +145,7 @@
         lanes = pl.ds(lo, hi - lo)
         waits = [
             links.send(O.at[q, rs, lanes], land.at[i], land.at[i], dev, 0)
-            for i, (q, dev) in enumerate(((xp, dxp), (xm, dxm), (xo, dxo)))
+            for i, (q, dev) in enumerate(((xo, dxo), (xp, dxp), (xm, dxm)))
         ]
         yield
         for wait in waits:
@@ -209,17 +209,33 @@
     bx.append(straight(pl.ds(*CHUNKS[-1]), LA, QL, xb))
     bz = along_z(x, None, LA, QL, zb, 0)
     ax = straight(rows(0), 0, LA, xa)
-    ring_steps(*az, bx[4], bx[3], bx[2])
-    yield
-    ring_steps(bx[4], bz, *az, bx[3], bx[1])
-    yield
-    ring_steps(*az, bx[3], bz, bx[2], bx[0])
-    yield
-    ring_steps(*az, bx[2], bz, bx[1])
-    yield
-    ring_steps(*az, ax, bx[1], bz, bx[0])
-    yield
-    ring_steps(bx[0], bz, ax)
+    ring_steps(*az)
+    yield
+    ring_steps(bx[4], bx[3])
+    yield
+    ring_steps(bx[2])
+    yield
+    ring_steps(*az)
+    yield
+    ring_steps(bx[4], bz, bx[3])
+    yield
+    ring_steps(bx[1])
+    yield
+    ring_steps(*az)
+    yield
+    ring_steps(bx[3], bz, bx[2])
+    yield
+    ring_steps(bx[0])
+    yield
+    ring_steps(*az)
+    yield
+    ring_steps(bx[2], bz, bx[1])
+    yield
+    ring_steps(*az, ax)
+    yield
+    ring_steps(bx[1], bz, bx[0])
+    yield
+    ring_steps(bx[0], ax, bz)
 
 
 def kernel(
@@ -337,7 +353,7 @@
     pl.semaphore_wait(barrier, 18 - 3 * ((NX - turn) // NX))
 
     def exchange_out():
-        for k in range(HOSTS):
+        for k in (4, 3, 5, 2, 6, 1, 7, 0):
             e = (h + k) % HOSTS
             copy = pltpu.make_async_remote_copy(
                 src_ref=msend.at[e], dst_ref=mrecv.at[hr, x],
@@ -385,7 +401,7 @@
             parts.append(jnp.zeros((ROWS, 128), BF16))
             got = mm(into_msg, jnp.concatenate(parts, axis=0), 1, 0).astype(BF16)
             rsend[which, r] = got.reshape(NX, 32, 128)
-        for i in range(NX):
+        for i in (2, 1, 3, 0):
             for r in range(2):
                 xi = (x + i) % NX
                 copy = pltpu.make_async_remote_copy(
@@ -415,8 +431,11 @@
                 copy.wait_recv()
             else:
                 pl.when(other)(copy.wait_recv)
-        got = rrecv[which].reshape(HOSTS * 32, 128).astype(F32)
-        res = mm(table[...], got, 1, 0, HIGHEST).astype(BF16)
+        got = rrecv[which].reshape(HOSTS * 32, 128)
+        if which:
+            res = mm(table[...].astype(BF16), got, 1, 0).astype(BF16)
+        else:
+            res = mm(table[...], got.astype(F32), 1, 0, HIGHEST).astype(BF16)
         for j in range(TILES):
             out[:, 128 * j : 128 * j + 128] = res[16 * j : 16 * j + 16]
 
@@ -477,21 +496,25 @@
     for q in quarters:
         out_task(q)
     run_o = scatter(oo, land_o, links[3], place)
-    next(run_o)
+    run_b = scatter(ob, land_b, links[2], place)
+    ring_steps(run_o)
+    ring_steps(run_o)
+    ring_steps(run_o)
     ring_steps(run_d)
     for q in quarters:
         da_task(q)
     hidden_task()
     for q in quarters:
         back_task(q)
-    run_b = scatter(ob, land_b, links[2], place)
-    next(run_b)
+    ring_steps(run_b)
+    ring_steps(run_b)
+    ring_steps(run_b)
     tasks = [task(grad_task, i, q) for i in range(3) for q in quarters]
-    for _ in range(4):
+    for _ in range(10):
         ring_steps(run_o, run_b)
-        for t in tasks[:3]:
+        for t in tasks[:2]:
             t()
-        tasks = tasks[3:]
+        tasks = tasks[2:]
     ring_steps(run_o)
     return_out(0, oo)
     ring_steps(run_b)

time: 78.1 us -> 76.6 us (0.981)
  Pallas kernels: 77.4 us -> 75.8 us
    pallas_call x1, Pallas kernels: 74.5 us -> 73 us  [body(): pl.pallas_call(kernel, out_shape=[pltpu.VMEM(shape, BF16) for shape in sh...]
where the time goes in v4:
time: 76.6 us; the launch traced here: 76.5 us
  Pallas kernels  75.8 us (99%)
    pallas_call x1, Pallas kernels, body(): pl.pallas_call(kernel, out_shape=[pltpu.VMEM(shape, BF16) for shape in sh...  73 us
    pallas_call x1, Pallas kernels, body(): pl.pallas_call(write_out, out_shape=[jax.ShapeDtypeStruct(shape, BF16) fo...  2.84 us

profile of v4, /device:TPU:1, one launch (start us, length us, event | category | flops | bytes accessed | tf_op | source)
XLA Modules:
  0.0 76.5 jit_solution(118703066139483470)
XLA Ops:
  0.6 73.0 %shard_map.110 = (bf16[16,896]{1,0:T(8,128)(2,1)S(1)}, bf16[16,896]{1,0:T(8,128)(2,1)S(1)}, bf16[1,152,7168]{2,1,0:T(8,128)(2,1)S(1)}, bf16[1,152,7168]{2,1,0:T(8,128)(2,1)S(1)}, bf16[1,152,7168]{2,1,0:T(8,128)(2,1)S(1)}) custom-call(bf16[16,896]{1,0:T(8,128)(2,1)} %tok_hbm.1, bf16[16,896]{1,0:T(8,128)(2,1)} %cot_hbm.1, s32[2,16]{1,0:T(2,128)} %bitcast.2, ...), custom_call_target="tpu_custom_call" | custom-call | tf_op jit(solution)/shard_map/pallas_call | solution.py:571
  73.6 2.8 %shard_map.111 = (bf16[16,896]{1,0:T(8,128)(2,1)}, bf16[16,896]{1,0:T(8,128)(2,1)}, bf16[1,152,7168]{2,1,0:T(8,128)(2,1)}, bf16[1,152,7168]{2,1,0:T(8,128)(2,1)}, bf16[1,152,7168]{2,1,0:T(8,128)(2,1)}) custom-call(bf16[16,896]{1,0:T(8,128)(2,1)S(1)} %get-tuple-element.10.refs_0_, bf16[16,896]{1,0:T(8,128)(2,1)S(1)} %get-tuple-element.11.refs_1_, ...), custom_call_target="tpu_custom_call" | custom-call | tf_op jit(solution)/shard_map/pallas_call | solution.py:592

commit v5 on v4

--- a/solution.py
+++ b/solution.py
@@ -209,7 +209,9 @@
     bx.append(straight(pl.ds(*CHUNKS[-1]), LA, QL, xb))
     bz = along_z(x, None, LA, QL, zb, 0)
     ax = straight(rows(0), 0, LA, xa)
-    ring_steps(*az)
+    ring_steps(az[0])
+    yield
+    ring_steps(az[1])
     yield
     ring_steps(bx[4], bx[3])
     yield
@@ -493,20 +495,22 @@
     for q in quarters:
         gate_task(q)
     act_task()
-    for q in quarters:
-        out_task(q)
     run_o = scatter(oo, land_o, links[3], place)
     run_b = scatter(ob, land_b, links[2], place)
-    ring_steps(run_o)
+    for half in range(2):
+        out_task(2 * half)
+        out_task(2 * half + 1)
+        ring_steps(run_o)
     ring_steps(run_o)
     ring_steps(run_o)
     ring_steps(run_d)
     for q in quarters:
         da_task(q)
     hidden_task()
-    for q in quarters:
-        back_task(q)
-    ring_steps(run_b)
+    for half in range(2):
+        back_task(2 * half)
+        back_task(2 * half + 1)
+        ring_steps(run_b)
     ring_steps(run_b)
     ring_steps(run_b)
     tasks = [task(grad_task, i, q) for i in range(3) for q in quarters]
@@ -548,7 +552,13 @@
 
 def write_out(*refs):
     parts, outs, sem = refs[:5], refs[5:10], refs[10]
-    copies = [pltpu.make_async_copy(parts[i], outs[i], sem.at[i]) for i in range(5)]
+    copies = []
+    for i in range(2, 5):
+        for q in range(NX):
+            piece = (slice(None), slice(None), pl.ds(q * QL, QL))
+            copies.append((parts[i].at[piece], outs[i].at[piece]))
+    copies += [(parts[i], outs[i]) for i in range(2)]
+    copies = [pltpu.make_async_copy(*pair, sem.at[n]) for n, pair in enumerate(copies)]
     for copy in copies:
         copy.start()
     for copy in copies:
@@ -594,7 +604,7 @@
         out_shape=[jax.ShapeDtypeStruct(shape, BF16) for shape in shapes],
         in_specs=[vmem] * 5,
         out_specs=[hbm] * 5,
-        scratch_shapes=[pltpu.SemaphoreType.DMA((5,))],
+        scratch_shapes=[pltpu.SemaphoreType.DMA((3 * NX + 2,))],
         compiler_params=pltpu.CompilerParams(vmem_limit_bytes=1024 * 1024),
     )(*[pltpu.with_memory_space_constraint(part, pltpu.VMEM) for part in parts])
 

time: 76.6 us -> 76.9 us (level)
  no operation moved by 1% of the time
where the time goes in v5:
time: 76.9 us; the launch traced here: 76.8 us
  Pallas kernels  76.2 us (99%)
    pallas_call x1, Pallas kernels, body(): pl.pallas_call(kernel, out_shape=[pltpu.VMEM(shape, BF16) for shape in sh...  73.3 us
    pallas_call x1, Pallas kernels, body(): pl.pallas_call(write_out, out_shape=[jax.ShapeDtypeStruct(shape, BF16) fo...  2.86 us

profile of v5, /device:TPU:1, one launch (start us, length us, event | category | flops | bytes accessed | tf_op | source)
XLA Modules:
  0.0 76.8 jit_solution(3801415356210347081)
XLA Ops:
  0.6 73.3 %shard_map.110 = (bf16[16,896]{1,0:T(8,128)(2,1)S(1)}, bf16[16,896]{1,0:T(8,128)(2,1)S(1)}, bf16[1,152,7168]{2,1,0:T(8,128)(2,1)S(1)}, bf16[1,152,7168]{2,1,0:T(8,128)(2,1)S(1)}, bf16[1,152,7168]{2,1,0:T(8,128)(2,1)S(1)}) custom-call(bf16[16,896]{1,0:T(8,128)(2,1)} %tok_hbm.1, bf16[16,896]{1,0:T(8,128)(2,1)} %cot_hbm.1, s32[2,16]{1,0:T(2,128)} %bitcast.2, ...), custom_call_target="tpu_custom_call" | custom-call | tf_op jit(solution)/shard_map/pallas_call | solution.py:581
  73.9 2.9 %shard_map.111 = (bf16[16,896]{1,0:T(8,128)(2,1)}, bf16[16,896]{1,0:T(8,128)(2,1)}, bf16[1,152,7168]{2,1,0:T(8,128)(2,1)}, bf16[1,152,7168]{2,1,0:T(8,128)(2,1)}, bf16[1,152,7168]{2,1,0:T(8,128)(2,1)}) custom-call(bf16[16,896]{1,0:T(8,128)(2,1)S(1)} %get-tuple-element.10.refs_0_, bf16[16,896]{1,0:T(8,128)(2,1)S(1)} %get-tuple-element.11.refs_1_, ...), custom_call_target="tpu_custom_call" | custom-call | tf_op jit(solution)/shard_map/pallas_call | solution.py:602
